TPU v7x, 256 devices: a whole 4x4x8 slice. The times are simulated.
256 devices in a mesh: segment: 2 (over core), row: 4 (over x), col: 32 (over y, z).
Axes of the slice: x: 4, y: 4, z: 8, core: 2. Of those that a mesh axis runs over, the one named last changes fastest.
Arguments:
- images: bfloat16 [6, 32, 4096, 512], P(None, 'row', 'col'), may hold values from -6 to 6
- tissue_list: int32 [6, 64], replicated, may hold values from 0 to 63, as said below
- tissue_count: int32 [6], replicated, may hold values from 1 to 64
- w_reduce: bfloat16 [2, 512, 128], P('segment'), may hold values from -0.25 to 0.25
- w_spatial: bfloat16 [2, 3, 3, 128, 128], P('segment'), may hold values from -0.1875 to 0.1875
- w_expand: bfloat16 [2, 128, 512], P('segment'), may hold values from -0.5 to 0.5
- inner_gain: bfloat16 [2, 2, 128], P('segment'), may hold values from 0.25 to 1.75
- inner_bias: bfloat16 [2, 2, 128], P('segment'), may hold values from -3 to 3
- outer_gain: bfloat16 [2, 512], P('segment'), may hold values from 0.25 to 1.75
- outer_bias: bfloat16 [2, 512], P('segment'), may hold values from -3 to 3
Outputs:
- features: bfloat16 [6, 32, 4096, 512], P('segment', 'row', 'col')
Inputs may be any that keep to these rules, and one draw needn't show every extreme that they name: `tissue_list`: the first tissue_count[m] entries of row m are distinct tile indices in ascending order; the entries after them are arbitrary tile indices.
All inputs are finite; a program needn't handle non-finite values.
Results may differ from a plain program's by a relative error of at most 0.0065.
Values may be sent and summed in bfloat16 or wider, within the bound.
A program may use at most 64 MiB of HBM per device.

v0:
```python
import jax
import jax.numpy as jnp
from jax import lax
from jax.sharding import PartitionSpec as P

TW = 64
TILES_DEV = 2


def extended(cells, sides, width):
    for axis, dim in sides:
        count = lax.axis_size(axis)
        ends = count - 1
        head = lax.slice_in_dim(cells, 0, width, axis=dim)
        tail = lax.slice_in_dim(cells, cells.shape[dim] - width, cells.shape[dim], axis=dim)
        cells = jnp.concatenate(
            [
                lax.ppermute(tail, axis, [(i, (i + 1) % count) for i in range(ends)]),
                cells,
                lax.ppermute(head, axis, [((i + 1) % count, i) for i in range(ends)]),
            ],
            axis=dim,
        )
    return cells


def from_behind(value, axis, steps):
    count = lax.axis_size(axis)
    initial, last = (max(0, -steps), min(count, count - steps))
    return lax.ppermute(value, axis, [(source, source + steps) for source in range(initial, last)])


def run_block(x, mask_tiles, params):
    w_red, w_spa, w_exp, in_gain, in_bias, out_gain, out_bias = params
    rows, width, chans = x.shape
    inner = w_red.shape[1]
    mask_cols = jnp.repeat(mask_tiles, TW)[None, :, None]
    v = jnp.dot(x.reshape(-1, chans), w_red, preferred_element_type=jnp.float32)
    v = jax.nn.relu(v * in_gain[0].astype(jnp.float32) + in_bias[0].astype(jnp.float32))
    reduced = (v.reshape(rows, width, inner) * mask_cols).astype(jnp.bfloat16)
    padded = extended(reduced, (("row", 0), ("col", 1)), 1)
    total = jnp.zeros((rows * width, inner), jnp.float32)
    for dy in range(3):
        for dx in range(3):
            window = padded[dy : dy + rows, dx : dx + width].reshape(-1, inner)
            total = total + jnp.dot(window, w_spa[dy, dx], preferred_element_type=jnp.float32)
    spatial = jax.nn.relu(
        total * in_gain[1].astype(jnp.float32) + in_bias[1].astype(jnp.float32)
    ).astype(jnp.bfloat16)
    z = jnp.dot(spatial, w_exp, preferred_element_type=jnp.float32)
    z = (
        z * out_gain.astype(jnp.float32)
        + out_bias.astype(jnp.float32)
        + x.reshape(-1, chans).astype(jnp.float32)
    )
    z = jax.nn.relu(z).reshape(rows, width, chans) * mask_cols
    return z.astype(jnp.bfloat16)


def shards(
    images,
    tissue_list,
    tissue_count,
    w_reduce,
    w_spatial,
    w_expand,
    inner_gain,
    inner_bias,
    outer_gain,
    outer_bias,
):
    segment_here = lax.axis_index("segment")
    first = segment_here == 0
    tiles_here = lax.axis_index("col") * TILES_DEV + jnp.arange(TILES_DEV, dtype=jnp.int32)
    listed_pos = jnp.arange(tissue_list.shape[1], dtype=jnp.int32)
    valid = listed_pos[None, :] < tissue_count[:, None]
    hit = (tissue_list[:, :, None] == tiles_here[None, None, :]) & valid[:, :, None]
    masks = jnp.any(hit, axis=1).astype(jnp.float32)
    total_slides = images.shape[0]
    half = total_slides // 2
    params = (w_reduce, w_spatial, w_expand, inner_gain, inner_bias, outer_gain, outer_bias)
    own = tuple((p[0] for p in params))
    received = jnp.zeros_like(images[0])
    results = []
    for tick in range(total_slides + 1):
        source = min(tick, total_slides - 1)
        current = jnp.where(first, images[source], received)
        slot = jnp.where(first, source, max(tick - 1, 0))
        result = run_block(current, masks[slot], own)
        if tick >= 1:
            results.append(result)
        if tick < total_slides:
            received = from_behind(result, "segment", 1)
    upper = jnp.stack(results[half:])
    lower = jnp.stack(results[:half])
    returned = from_behind(lower, "segment", -1)
    return jnp.where(first, returned, upper)


def solution(mesh):
    placed = (
        P(None, "row", "col", None),
        P(),
        P(),
        P("segment", None, None),
        P("segment", None, None, None, None),
        P("segment", None, None),
        P("segment", None, None),
        P("segment", None, None),
        P("segment", None),
        P("segment", None),
    )
    return jax.shard_map(
        shards,
        mesh=mesh,
        in_specs=placed,
        out_specs=P("segment", "row", "col", None),
        check_vma=False,
    )
```

profile of v0, /device:TPU:24, one launch (start us, length us, event | category | flops | bytes accessed | tf_op | source)
XLA Modules:
  0.0 226.1 jit_solution(15109863594887962383)
XLA Ops:
  4.2 3.4 %collective-permute-start = (bf16[1,128,128]{2,1,0:T(8,128)(2,1)S(1)}, bf16[1,128,128]{2,1,0:T(8,128)(2,1)S(1)}, u32[]{:S(2)}, u32[]{:S(2)}) collective-permute-start(bf16[1,128,128]{2,1,0:T(8,128)(2,1)S(1)} %get-tuple-element.108), channel_id=1, source_target_pairs={{0,32},{32,64},{64,96},{1,33},{33,65},{65,97},{2,34},{34,66},{66,9... | collective-permute-start | bytes 98312 | tf_op jit(solution)/shard_map/ppermute | solution.py:18
  9.2 4.2 %collective-permute-done.1 = bf16[1,128,128]{2,1,0:T(8,128)(2,1)S(1)} collective-permute-done((bf16[1,128,128]{2,1,0:T(8,128)(2,1)S(1)}, bf16[1,128,128]{2,1,0:T(8,128)(2,1)S(1)}, u32[]{:S(2)}, u32[]{:S(2)}) %collective-permute-start.1) | collective-permute-done | bytes 32800 | tf_op jit(solution)/shard_map/ppermute | solution.py:20
  13.4 3.8 %collective-permute-start.2 = (bf16[10,1,128]{2,1,0:T(2,128)(2,1)S(1)}, bf16[10,1,128]{2,1,0:T(2,128)(2,1)S(1)}, u32[]{:S(2)}, u32[]{:S(2)}) collective-permute-start(bf16[10,1,128]{2,1,0:T(2,128)(2,1)S(1)} %get-tuple-element.80), channel_id=1, source_target_pairs={{0,1},{1,2},{2,3},{3,4},{4,5},{5,6},{6,7},{7,8},{8,9},{9,10},{10,1... | collective-permute-start | bytes 7688 | tf_op jit(solution)/shard_map/ppermute | solution.py:18
  17.3 6.0 %collective-permute-start.3 = (bf16[10,1,128]{2,1,0:T(2,128)(2,1)S(1)}, bf16[10,1,128]{2,1,0:T(2,128)(2,1)S(1)}, u32[]{:S(2)}, u32[]{:S(2)}) collective-permute-start(bf16[10,1,128]{2,1,0:T(2,128)(2,1)S(1)} %get-tuple-element.81), channel_id=1, source_target_pairs={{1,0},{2,1},{3,2},{4,3},{5,4},{6,5},{7,6},{8,7},{9,8},{10,9},{11,1... | collective-permute-start | bytes 7688 | tf_op jit(solution)/shard_map/ppermute | solution.py:20
  26.6 2.0 add_maximum_fusion.6
  28.6 1.9 multiply_convert_fusion.11
  32.0 2.0 collective-permute-done.4
  36.0 3.4 %collective-permute-start.5 = (bf16[1,128,128]{2,1,0:T(8,128)(2,1)S(1)}, bf16[1,128,128]{2,1,0:T(8,128)(2,1)S(1)}, u32[]{:S(2)}, u32[]{:S(2)}) collective-permute-start(bf16[1,128,128]{2,1,0:T(8,128)(2,1)S(1)} %get-tuple-element.104), channel_id=1, source_target_pairs={{0,32},{32,64},{64,96},{1,33},{33,65},{65,97},{2,34},{34,66},{66,9... | collective-permute-start | bytes 98312 | tf_op jit(solution)/shard_map/ppermute | solution.py:18
  41.0 4.2 %collective-permute-done.6 = bf16[1,128,128]{2,1,0:T(8,128)(2,1)S(1)} collective-permute-done((bf16[1,128,128]{2,1,0:T(8,128)(2,1)S(1)}, bf16[1,128,128]{2,1,0:T(8,128)(2,1)S(1)}, u32[]{:S(2)}, u32[]{:S(2)}) %collective-permute-start.6) | collective-permute-done | bytes 32800 | tf_op jit(solution)/shard_map/ppermute | solution.py:20
  45.3 2.0 collective-permute-start.7
  47.3 6.2 %collective-permute-start.8 = (bf16[10,1,128]{2,1,0:T(2,128)(2,1)S(1)}, bf16[10,1,128]{2,1,0:T(2,128)(2,1)S(1)}, u32[]{:S(2)}, u32[]{:S(2)}) collective-permute-start(bf16[10,1,128]{2,1,0:T(2,128)(2,1)S(1)} %get-tuple-element.77), channel_id=1, source_target_pairs={{1,0},{2,1},{3,2},{4,3},{5,4},{6,5},{7,6},{8,7},{9,8},{10,9},{11,1... | collective-permute-start | bytes 7688 | tf_op jit(solution)/shard_map/ppermute | solution.py:20
  57.7 2.0 add_maximum_fusion.5
  61.0 2.3 %collective-permute-start.9 = (bf16[8,128,512]{2,1,0:T(8,128)(2,1)}, bf16[8,128,512]{2,1,0:T(8,128)(2,1)}, u32[]{:S(2)}, u32[]{:S(2)}) collective-permute-start(bf16[8,128,512]{2,1,0:T(8,128)(2,1)} %multiply_convert_fusion.9), channel_id=1, source_target_pairs={{0,128},{1,129},{2,130},{3,131},{4,132},{5,133},{6,134},{7,135},{8... | collective-permute-start | bytes 3145736 | tf_op jit(solution)/shard_map/ppermute | solution.py:30
  66.9 3.1 %collective-permute-start.10 = (bf16[1,128,128]{2,1,0:T(8,128)(2,1)S(1)}, bf16[1,128,128]{2,1,0:T(8,128)(2,1)S(1)}, u32[]{:S(2)}, u32[]{:S(2)}) collective-permute-start(bf16[1,128,128]{2,1,0:T(8,128)(2,1)S(1)} %get-tuple-element.100), channel_id=1, source_target_pairs={{0,32},{32,64},{64,96},{1,33},{33,65},{65,97},{2,34},{34,66},{66,9... | collective-permute-start | bytes 98312 | tf_op jit(solution)/shard_map/ppermute | solution.py:18
  71.5 4.2 %collective-permute-done.11 = bf16[1,128,128]{2,1,0:T(8,128)(2,1)S(1)} collective-permute-done((bf16[1,128,128]{2,1,0:T(8,128)(2,1)S(1)}, bf16[1,128,128]{2,1,0:T(8,128)(2,1)S(1)}, u32[]{:S(2)}, u32[]{:S(2)}) %collective-permute-start.11) | collective-permute-done | bytes 32800 | tf_op jit(solution)/shard_map/ppermute | solution.py:20
  75.8 4.1 %collective-permute-start.12 = (bf16[10,1,128]{2,1,0:T(2,128)(2,1)S(1)}, bf16[10,1,128]{2,1,0:T(2,128)(2,1)S(1)}, u32[]{:S(2)}, u32[]{:S(2)}) collective-permute-start(bf16[10,1,128]{2,1,0:T(2,128)(2,1)S(1)} %get-tuple-element.72), channel_id=1, source_target_pairs={{0,1},{1,2},{2,3},{3,4},{4,5},{5,6},{6,7},{7,8},{8,9},{9,10},{10,1... | collective-permute-start | bytes 7688 | tf_op jit(solution)/shard_map/ppermute | solution.py:18
  79.9 4.2 %collective-permute-start.13 = (bf16[10,1,128]{2,1,0:T(2,128)(2,1)S(1)}, bf16[10,1,128]{2,1,0:T(2,128)(2,1)S(1)}, u32[]{:S(2)}, u32[]{:S(2)}) collective-permute-start(bf16[10,1,128]{2,1,0:T(2,128)(2,1)S(1)} %get-tuple-element.73), channel_id=1, source_target_pairs={{1,0},{2,1},{3,2},{4,3},{5,4},{6,5},{7,6},{8,7},{9,8},{10,9},{11,1... | collective-permute-start | bytes 7688 | tf_op jit(solution)/shard_map/ppermute | solution.py:20
  88.3 3.3 %add_maximum_fusion.4 = f32[1024,512]{1,0:T(8,128)} fusion(bf16[1024,512]{1,0:T(8,128)(2,1)} %bitcast.385, f32[1024,128]{1,0:T(8,128)S(1)} %fusion.102, f32[1024,128]{1,0:T(8,128)} %convolution_add_fusion.29, bf16[1024,128]{1,0:T(8,128)(2,1)S(1)} %bitcast.402, f32[512]{0:T(512)S(1)} %bitcast.464, f32[512]{0:T(512)S(1)} %bitcast.457, ...), kind=kOutput, calls=%fused_computation.15 | convolution fusion | flops 171180032 | bytes 4625408 | tf_op jit(solution)/shard_map/dot_general | solution.py:50
  91.6 2.9 %multiply_convert_fusion.7 = bf16[8,128,512]{2,1,0:T(8,128)(2,1)} fusion(f32[8,128,512]{2,1,0:T(8,128)} %bitcast.305, f32[128]{0:T(128)S(1)} %mul.424), kind=kLoop, calls=%fused_computation.13 | loop fusion | flops 1048576 | bytes 3146240 | tf_op jit(solution)/shard_map/convert_element_type | solution.py:57
  94.5 2.3 collective-permute-start.14
  100.3 2.0 collective-permute-start.15
  103.9 4.2 %collective-permute-done.16 = bf16[1,128,128]{2,1,0:T(8,128)(2,1)S(1)} collective-permute-done((bf16[1,128,128]{2,1,0:T(8,128)(2,1)S(1)}, bf16[1,128,128]{2,1,0:T(8,128)(2,1)S(1)}, u32[]{:S(2)}, u32[]{:S(2)}) %collective-permute-start.16) | collective-permute-done | bytes 32800 | tf_op jit(solution)/shard_map/ppermute | solution.py:20
  108.2 3.9 %collective-permute-start.17 = (bf16[10,1,128]{2,1,0:T(2,128)(2,1)S(1)}, bf16[10,1,128]{2,1,0:T(2,128)(2,1)S(1)}, u32[]{:S(2)}, u32[]{:S(2)}) collective-permute-start(bf16[10,1,128]{2,1,0:T(2,128)(2,1)S(1)} %get-tuple-element.68), channel_id=1, source_target_pairs={{0,1},{1,2},{2,3},{3,4},{4,5},{5,6},{6,7},{7,8},{8,9},{9,10},{10,1... | collective-permute-start | bytes 7688 | tf_op jit(solution)/shard_map/ppermute | solution.py:18
  112.1 4.4 %collective-permute-start.18 = (bf16[10,1,128]{2,1,0:T(2,128)(2,1)S(1)}, bf16[10,1,128]{2,1,0:T(2,128)(2,1)S(1)}, u32[]{:S(2)}, u32[]{:S(2)}) collective-permute-start(bf16[10,1,128]{2,1,0:T(2,128)(2,1)S(1)} %get-tuple-element.69), channel_id=1, source_target_pairs={{1,0},{2,1},{3,2},{4,3},{5,4},{6,5},{7,6},{8,7},{9,8},{10,9},{11,1... | collective-permute-start | bytes 7688 | tf_op jit(solution)/shard_map/ppermute | solution.py:20
  120.5 3.3 %add_maximum_fusion.3 = f32[1024,512]{1,0:T(8,128)} fusion(bf16[1024,512]{1,0:T(8,128)(2,1)} %bitcast.387, f32[1024,128]{1,0:T(8,128)S(1)} %fusion.101, f32[1024,128]{1,0:T(8,128)} %convolution_add_fusion.22, bf16[1024,128]{1,0:T(8,128)(2,1)S(1)} %bitcast.403, f32[512]{0:T(512)S(1)} %bitcast.465, f32[512]{0:T(512)S(1)} %bitcast.458, ...), kind=kOutput, calls=%fused_computation.12 | convolution fusion | flops 171180032 | bytes 4625408 | tf_op jit(solution)/shard_map/dot_general | solution.py:50
  123.8 2.9 %multiply_convert_fusion.5 = bf16[8,128,512]{2,1,0:T(8,128)(2,1)} fusion(f32[8,128,512]{2,1,0:T(8,128)} %bitcast.307, f32[128]{0:T(128)S(1)} %mul.438), kind=kLoop, calls=%fused_computation.10 | loop fusion | flops 1048576 | bytes 3146240 | tf_op jit(solution)/shard_map/convert_element_type | solution.py:57
  126.8 2.2 collective-permute-start.20
  132.6 2.0 collective-permute-start.21
  136.2 4.2 %collective-permute-done.22 = bf16[1,128,128]{2,1,0:T(8,128)(2,1)S(1)} collective-permute-done((bf16[1,128,128]{2,1,0:T(8,128)(2,1)S(1)}, bf16[1,128,128]{2,1,0:T(8,128)(2,1)S(1)}, u32[]{:S(2)}, u32[]{:S(2)}) %collective-permute-start.22) | collective-permute-done | bytes 32800 | tf_op jit(solution)/shard_map/ppermute | solution.py:20
  140.4 3.1 %collective-permute-start.23 = (bf16[10,1,128]{2,1,0:T(2,128)(2,1)S(1)}, bf16[10,1,128]{2,1,0:T(2,128)(2,1)S(1)}, u32[]{:S(2)}, u32[]{:S(2)}) collective-permute-start(bf16[10,1,128]{2,1,0:T(2,128)(2,1)S(1)} %get-tuple-element.64), channel_id=1, source_target_pairs={{0,1},{1,2},{2,3},{3,4},{4,5},{5,6},{6,7},{7,8},{8,9},{9,10},{10,1... | collective-permute-start | bytes 7688 | tf_op jit(solution)/shard_map/ppermute | solution.py:18
  143.5 5.2 %collective-permute-start.24 = (bf16[10,1,128]{2,1,0:T(2,128)(2,1)S(1)}, bf16[10,1,128]{2,1,0:T(2,128)(2,1)S(1)}, u32[]{:S(2)}, u32[]{:S(2)}) collective-permute-start(bf16[10,1,128]{2,1,0:T(2,128)(2,1)S(1)} %get-tuple-element.65), channel_id=1, source_target_pairs={{1,0},{2,1},{3,2},{4,3},{5,4},{6,5},{7,6},{8,7},{9,8},{10,9},{11,1... | collective-permute-start | bytes 7688 | tf_op jit(solution)/shard_map/ppermute | solution.py:20
  152.8 3.4 %add_maximum_fusion.2 = f32[1024,512]{1,0:T(8,128)} fusion(bf16[1024,512]{1,0:T(8,128)(2,1)} %bitcast.389, f32[1024,128]{1,0:T(8,128)S(1)} %fusion.100, f32[1024,128]{1,0:T(8,128)} %convolution_add_fusion.15, bf16[1024,128]{1,0:T(8,128)(2,1)S(1)} %bitcast.404, f32[512]{0:T(512)S(1)} %bitcast.466, f32[512]{0:T(512)S(1)} %bitcast.459, ...), kind=kOutput, calls=%fused_computation.9 | convolution fusion | flops 171180032 | bytes 4625408 | tf_op jit(solution)/shard_map/dot_general | solution.py:50
  156.2 2.9 %multiply_convert_fusion.3 = bf16[8,128,512]{2,1,0:T(8,128)(2,1)} fusion(f32[8,128,512]{2,1,0:T(8,128)} %bitcast.309, f32[128]{0:T(128)S(1)} %mul.452), kind=kLoop, calls=%fused_computation.7 | loop fusion | flops 1048576 | bytes 3146240 | tf_op jit(solution)/shard_map/convert_element_type | solution.py:57
  159.1 2.3 %collective-permute-start.25 = (bf16[8,128,512]{2,1,0:T(8,128)(2,1)}, bf16[8,128,512]{2,1,0:T(8,128)(2,1)}, u32[]{:S(2)}, u32[]{:S(2)}) collective-permute-start(bf16[8,128,512]{2,1,0:T(8,128)(2,1)} %multiply_convert_fusion.3), channel_id=1, source_target_pairs={{0,128},{1,129},{2,130},{3,131},{4,132},{5,133},{6,134},{7,135},{8... | collective-permute-start | bytes 3145736 | tf_op jit(solution)/shard_map/ppermute | solution.py:30
  164.9 2.0 collective-permute-start.26
  169.6 3.2 %collective-permute-done.27 = bf16[1,128,128]{2,1,0:T(8,128)(2,1)S(1)} collective-permute-done((bf16[1,128,128]{2,1,0:T(8,128)(2,1)S(1)}, bf16[1,128,128]{2,1,0:T(8,128)(2,1)S(1)}, u32[]{:S(2)}, u32[]{:S(2)}) %collective-permute-start.27) | collective-permute-done | bytes 32800 | tf_op jit(solution)/shard_map/ppermute | solution.py:20
  172.8 2.2 collective-permute-start.28
  174.9 6.0 %collective-permute-start.29 = (bf16[10,1,128]{2,1,0:T(2,128)(2,1)S(1)}, bf16[10,1,128]{2,1,0:T(2,128)(2,1)S(1)}, u32[]{:S(2)}, u32[]{:S(2)}) collective-permute-start(bf16[10,1,128]{2,1,0:T(2,128)(2,1)S(1)} %get-tuple-element.61), channel_id=1, source_target_pairs={{1,0},{2,1},{3,2},{4,3},{5,4},{6,5},{7,6},{8,7},{9,8},{10,9},{11,1... | collective-permute-start | bytes 7688 | tf_op jit(solution)/shard_map/ppermute | solution.py:20
  184.8 2.0 add_maximum_fusion.1
  186.8 2.1 multiply_convert_fusion.1
  191.9 2.0 pad_maximum_fusion
  198.6 2.1 collective-permute-start.31
  203.3 3.2 %collective-permute-done.32 = bf16[1,128,128]{2,1,0:T(8,128)(2,1)S(1)} collective-permute-done((bf16[1,128,128]{2,1,0:T(8,128)(2,1)S(1)}, bf16[1,128,128]{2,1,0:T(8,128)(2,1)S(1)}, u32[]{:S(2)}, u32[]{:S(2)}) %collective-permute-start.32) | collective-permute-done | bytes 32800 | tf_op jit(solution)/shard_map/ppermute | solution.py:20
  206.5 1.9 collective-permute-start.33
  208.5 6.5 %collective-permute-start.34 = (bf16[10,1,128]{2,1,0:T(2,128)(2,1)S(1)}, bf16[10,1,128]{2,1,0:T(2,128)(2,1)S(1)}, u32[]{:S(2)}, u32[]{:S(2)}) collective-permute-start(bf16[10,1,128]{2,1,0:T(2,128)(2,1)S(1)} %get-tuple-element.57), channel_id=1, source_target_pairs={{1,0},{2,1},{3,2},{4,3},{5,4},{6,5},{7,6},{8,7},{9,8},{10,9},{11,1... | collective-permute-start | bytes 7688 | tf_op jit(solution)/shard_map/ppermute | solution.py:20
  218.6 2.0 add_maximum_fusion
  220.6 2.1 multiply_convert_fusion
  222.8 3.3 %maximum_select_fusion = bf16[3,8,128,512]{3,2,1,0:T(8,128)(2,1)} fusion(bf16[3,8,128,512]{3,2,1,0:T(8,128)(2,1)} %collective-permute-done.19, bf16[1,8,128,512]{3,2,1,0:T(8,128)(2,1)S(1)} %multiply_convert_fusion, bf16[1,8,128,512]{3,2,1,0:T(8,128)(2,1)S(1)} %copy-done.16, bf16[1,8,128,512]{3,2,1,0:T(8,128)(2,1)S(1)} %copy-done.15, pred[]{:T(512)S(6)} %eq.16), kind=kLoop, calls=%fused_computation.1 | loop fusion | flops 4718592 | bytes 9437185 | tf_op jit(solution)/shard_map/jit(_where)/select_n | solution.py:97
  (235 shorter events, 70.5 us)
Async XLA Ops:
  0.0 26.6 %copy-start = (bf16[1,128,512]{2,1,0:T(8,128)(2,1)S(1)}, bf16[1,128,512]{2,1,0:T(8,128)(2,1)}, u32[]{:S(2)}) copy-start(bf16[1,128,512]{2,1,0:T(8,128)(2,1)} %param.15) | copy-start | bytes 393220
  0.0 3.6 %copy-start.14 = (bf16[1,512,128]{2,1,0:T(8,128)(2,1)S(1)}, bf16[1,512,128]{2,1,0:T(8,128)(2,1)}, u32[]{:S(2)}) copy-start(bf16[1,512,128]{2,1,0:T(8,128)(2,1)} %param.13) | copy-start | bytes 393220
  2.2 6.7 %copy-start.18 = (bf16[1,512]{1,0:T(2,128)(2,1)S(1)}, bf16[1,512]{1,0:T(2,128)(2,1)}, u32[]{:S(2)}) copy-start(bf16[1,512]{1,0:T(2,128)(2,1)} %param.18) | copy-start | bytes 3076
  2.2 6.7 %copy-start.19 = (bf16[1,512]{1,0:T(2,128)(2,1)S(1)}, bf16[1,512]{1,0:T(2,128)(2,1)}, u32[]{:S(2)}) copy-start(bf16[1,512]{1,0:T(2,128)(2,1)} %param.19) | copy-start | bytes 3076
  3.6 19.8 %copy-start.5 = (bf16[1,3,3,128,128]{4,3,2,1,0:T(8,128)(2,1)S(1)}, bf16[1,3,3,128,128]{4,3,2,1,0:T(8,128)(2,1)}, u32[]{:S(2)}) copy-start(bf16[1,3,3,128,128]{4,3,2,1,0:T(8,128)(2,1)} %param.14) | copy-start | bytes 884740
  4.2 5.0 %collective-permute-start = (bf16[1,128,128]{2,1,0:T(8,128)(2,1)S(1)}, bf16[1,128,128]{2,1,0:T(8,128)(2,1)S(1)}, u32[]{:S(2)}, u32[]{:S(2)}) collective-permute-start(bf16[1,128,128]{2,1,0:T(8,128)(2,1)S(1)} %get-tuple-element.108), channel_id=1, source_target_pairs={{0,32},{32,64},{64,96},{1,33},{33,65},{65,97},{2,34},{34,66},{66,9... | collective-permute-start | bytes 98312 | tf_op jit(solution)/shard_map/ppermute | solution.py:18
  7.6 5.8 %collective-permute-start.1 = (bf16[1,128,128]{2,1,0:T(8,128)(2,1)S(1)}, bf16[1,128,128]{2,1,0:T(8,128)(2,1)S(1)}, u32[]{:S(2)}, u32[]{:S(2)}) collective-permute-start(bf16[1,128,128]{2,1,0:T(8,128)(2,1)S(1)} %get-tuple-element.109), channel_id=1, source_target_pairs={{32,0},{64,32},{96,64},{33,1},{65,33},{97,65},{34,2},{66,34},{98,6... | collective-permute-start | bytes 98312 | tf_op jit(solution)/shard_map/ppermute | solution.py:20
  13.4 10.1 %collective-permute-start.2 = (bf16[10,1,128]{2,1,0:T(2,128)(2,1)S(1)}, bf16[10,1,128]{2,1,0:T(2,128)(2,1)S(1)}, u32[]{:S(2)}, u32[]{:S(2)}) collective-permute-start(bf16[10,1,128]{2,1,0:T(2,128)(2,1)S(1)} %get-tuple-element.80), channel_id=1, source_target_pairs={{0,1},{1,2},{2,3},{3,4},{4,5},{5,6},{6,7},{7,8},{8,9},{9,10},{10,1... | collective-permute-start | bytes 7688 | tf_op jit(solution)/shard_map/ppermute | solution.py:18
  17.3 7.4 %collective-permute-start.3 = (bf16[10,1,128]{2,1,0:T(2,128)(2,1)S(1)}, bf16[10,1,128]{2,1,0:T(2,128)(2,1)S(1)}, u32[]{:S(2)}, u32[]{:S(2)}) collective-permute-start(bf16[10,1,128]{2,1,0:T(2,128)(2,1)S(1)} %get-tuple-element.81), channel_id=1, source_target_pairs={{1,0},{2,1},{3,2},{4,3},{5,4},{6,5},{7,6},{8,7},{9,8},{10,9},{11,1... | collective-permute-start | bytes 7688 | tf_op jit(solution)/shard_map/ppermute | solution.py:20
  30.5 3.6 %collective-permute-start.4 = (bf16[8,128,512]{2,1,0:T(8,128)(2,1)S(1)}, bf16[8,128,512]{2,1,0:T(8,128)(2,1)S(1)}, u32[]{:S(2)}, u32[]{:S(2)}) collective-permute-start(bf16[8,128,512]{2,1,0:T(8,128)(2,1)S(1)} %multiply_convert_fusion.11), channel_id=1, source_target_pairs={{0,128},{1,129},{2,130},{3,131},{4,132},{5,133},{6,134},{7,135},{8... | collective-permute-start | bytes 3145736 | tf_op jit(solution)/shard_map/ppermute | solution.py:30
  35.4 18.3 %copy-start.10 = (bf16[8,128,512]{2,1,0:T(8,128)(2,1)}, bf16[8,128,512]{2,1,0:T(8,128)(2,1)S(1)}, u32[]{:S(2)}) copy-start(bf16[8,128,512]{2,1,0:T(8,128)(2,1)S(1)} %bitcast_select_fusion.5) | copy-start | bytes 3145732
  36.0 5.0 %collective-permute-start.5 = (bf16[1,128,128]{2,1,0:T(8,128)(2,1)S(1)}, bf16[1,128,128]{2,1,0:T(8,128)(2,1)S(1)}, u32[]{:S(2)}, u32[]{:S(2)}) collective-permute-start(bf16[1,128,128]{2,1,0:T(8,128)(2,1)S(1)} %get-tuple-element.104), channel_id=1, source_target_pairs={{0,32},{32,64},{64,96},{1,33},{33,65},{65,97},{2,34},{34,66},{66,9... | collective-permute-start | bytes 98312 | tf_op jit(solution)/shard_map/ppermute | solution.py:18
  39.4 5.8 %collective-permute-start.6 = (bf16[1,128,128]{2,1,0:T(8,128)(2,1)S(1)}, bf16[1,128,128]{2,1,0:T(8,128)(2,1)S(1)}, u32[]{:S(2)}, u32[]{:S(2)}) collective-permute-start(bf16[1,128,128]{2,1,0:T(8,128)(2,1)S(1)} %get-tuple-element.105), channel_id=1, source_target_pairs={{32,0},{64,32},{96,64},{33,1},{65,33},{97,65},{34,2},{66,34},{98,6... | collective-permute-start | bytes 98312 | tf_op jit(solution)/shard_map/ppermute | solution.py:20
  45.3 8.5 %collective-permute-start.7 = (bf16[10,1,128]{2,1,0:T(2,128)(2,1)S(1)}, bf16[10,1,128]{2,1,0:T(2,128)(2,1)S(1)}, u32[]{:S(2)}, u32[]{:S(2)}) collective-permute-start(bf16[10,1,128]{2,1,0:T(2,128)(2,1)S(1)} %get-tuple-element.76), channel_id=1, source_target_pairs={{0,1},{1,2},{2,3},{3,4},{4,5},{5,6},{6,7},{7,8},{8,9},{9,10},{10,1... | collective-permute-start | bytes 7688 | tf_op jit(solution)/shard_map/ppermute | solution.py:18
  47.3 7.6 %collective-permute-start.8 = (bf16[10,1,128]{2,1,0:T(2,128)(2,1)S(1)}, bf16[10,1,128]{2,1,0:T(2,128)(2,1)S(1)}, u32[]{:S(2)}, u32[]{:S(2)}) collective-permute-start(bf16[10,1,128]{2,1,0:T(2,128)(2,1)S(1)} %get-tuple-element.77), channel_id=1, source_target_pairs={{1,0},{2,1},{3,2},{4,3},{5,4},{6,5},{7,6},{8,7},{9,8},{10,9},{11,1... | collective-permute-start | bytes 7688 | tf_op jit(solution)/shard_map/ppermute | solution.py:20
  61.0 3.9 %collective-permute-start.9 = (bf16[8,128,512]{2,1,0:T(8,128)(2,1)}, bf16[8,128,512]{2,1,0:T(8,128)(2,1)}, u32[]{:S(2)}, u32[]{:S(2)}) collective-permute-start(bf16[8,128,512]{2,1,0:T(8,128)(2,1)} %multiply_convert_fusion.9), channel_id=1, source_target_pairs={{0,128},{1,129},{2,130},{3,131},{4,132},{5,133},{6,134},{7,135},{8... | collective-permute-start | bytes 3145736 | tf_op jit(solution)/shard_map/ppermute | solution.py:30
  66.3 18.0 %copy-start.11 = (bf16[8,128,512]{2,1,0:T(8,128)(2,1)}, bf16[8,128,512]{2,1,0:T(8,128)(2,1)S(1)}, u32[]{:S(2)}) copy-start(bf16[8,128,512]{2,1,0:T(8,128)(2,1)S(1)} %bitcast_select_fusion.4) | copy-start | bytes 3145732
  66.9 4.7 %collective-permute-start.10 = (bf16[1,128,128]{2,1,0:T(8,128)(2,1)S(1)}, bf16[1,128,128]{2,1,0:T(8,128)(2,1)S(1)}, u32[]{:S(2)}, u32[]{:S(2)}) collective-permute-start(bf16[1,128,128]{2,1,0:T(8,128)(2,1)S(1)} %get-tuple-element.100), channel_id=1, source_target_pairs={{0,32},{32,64},{64,96},{1,33},{33,65},{65,97},{2,34},{34,66},{66,9... | collective-permute-start | bytes 98312 | tf_op jit(solution)/shard_map/ppermute | solution.py:18
  70.0 5.8 %collective-permute-start.11 = (bf16[1,128,128]{2,1,0:T(8,128)(2,1)S(1)}, bf16[1,128,128]{2,1,0:T(8,128)(2,1)S(1)}, u32[]{:S(2)}, u32[]{:S(2)}) collective-permute-start(bf16[1,128,128]{2,1,0:T(8,128)(2,1)S(1)} %get-tuple-element.101), channel_id=1, source_target_pairs={{32,0},{64,32},{96,64},{33,1},{65,33},{97,65},{34,2},{66,34},{98,6... | collective-permute-start | bytes 98312 | tf_op jit(solution)/shard_map/ppermute | solution.py:20
  75.8 8.5 %collective-permute-start.12 = (bf16[10,1,128]{2,1,0:T(2,128)(2,1)S(1)}, bf16[10,1,128]{2,1,0:T(2,128)(2,1)S(1)}, u32[]{:S(2)}, u32[]{:S(2)}) collective-permute-start(bf16[10,1,128]{2,1,0:T(2,128)(2,1)S(1)} %get-tuple-element.72), channel_id=1, source_target_pairs={{0,1},{1,2},{2,3},{3,4},{4,5},{5,6},{6,7},{7,8},{8,9},{9,10},{10,1... | collective-permute-start | bytes 7688 | tf_op jit(solution)/shard_map/ppermute | solution.py:18
  79.9 5.5 %collective-permute-start.13 = (bf16[10,1,128]{2,1,0:T(2,128)(2,1)S(1)}, bf16[10,1,128]{2,1,0:T(2,128)(2,1)S(1)}, u32[]{:S(2)}, u32[]{:S(2)}) collective-permute-start(bf16[10,1,128]{2,1,0:T(2,128)(2,1)S(1)} %get-tuple-element.73), channel_id=1, source_target_pairs={{1,0},{2,1},{3,2},{4,3},{5,4},{6,5},{7,6},{8,7},{9,8},{10,9},{11,1... | collective-permute-start | bytes 7688 | tf_op jit(solution)/shard_map/ppermute | solution.py:20
  94.5 3.9 %collective-permute-start.14 = (bf16[8,128,512]{2,1,0:T(8,128)(2,1)}, bf16[8,128,512]{2,1,0:T(8,128)(2,1)}, u32[]{:S(2)}, u32[]{:S(2)}) collective-permute-start(bf16[8,128,512]{2,1,0:T(8,128)(2,1)} %multiply_convert_fusion.7), channel_id=1, source_target_pairs={{0,128},{1,129},{2,130},{3,131},{4,132},{5,133},{6,134},{7,135},{8... | collective-permute-start | bytes 3145736 | tf_op jit(solution)/shard_map/ppermute | solution.py:30
  99.8 17.0 %copy-start.12 = (bf16[8,128,512]{2,1,0:T(8,128)(2,1)}, bf16[8,128,512]{2,1,0:T(8,128)(2,1)S(1)}, u32[]{:S(2)}) copy-start(bf16[8,128,512]{2,1,0:T(8,128)(2,1)S(1)} %bitcast_select_fusion.3) | copy-start | bytes 3145732
  100.3 3.6 %collective-permute-start.15 = (bf16[1,128,128]{2,1,0:T(8,128)(2,1)S(1)}, bf16[1,128,128]{2,1,0:T(8,128)(2,1)S(1)}, u32[]{:S(2)}, u32[]{:S(2)}) collective-permute-start(bf16[1,128,128]{2,1,0:T(8,128)(2,1)S(1)} %get-tuple-element.96), channel_id=1, source_target_pairs={{0,32},{32,64},{64,96},{1,33},{33,65},{65,97},{2,34},{34,66},{66,9... | collective-permute-start | bytes 98312 | tf_op jit(solution)/shard_map/ppermute | solution.py:18
  102.3 5.8 %collective-permute-start.16 = (bf16[1,128,128]{2,1,0:T(8,128)(2,1)S(1)}, bf16[1,128,128]{2,1,0:T(8,128)(2,1)S(1)}, u32[]{:S(2)}, u32[]{:S(2)}) collective-permute-start(bf16[1,128,128]{2,1,0:T(8,128)(2,1)S(1)} %get-tuple-element.97), channel_id=1, source_target_pairs={{32,0},{64,32},{96,64},{33,1},{65,33},{97,65},{34,2},{66,34},{98,6... | collective-permute-start | bytes 98312 | tf_op jit(solution)/shard_map/ppermute | solution.py:20
  108.2 8.6 %collective-permute-start.17 = (bf16[10,1,128]{2,1,0:T(2,128)(2,1)S(1)}, bf16[10,1,128]{2,1,0:T(2,128)(2,1)S(1)}, u32[]{:S(2)}, u32[]{:S(2)}) collective-permute-start(bf16[10,1,128]{2,1,0:T(2,128)(2,1)S(1)} %get-tuple-element.68), channel_id=1, source_target_pairs={{0,1},{1,2},{2,3},{3,4},{4,5},{5,6},{6,7},{7,8},{8,9},{9,10},{10,1... | collective-permute-start | bytes 7688 | tf_op jit(solution)/shard_map/ppermute | solution.py:18
  112.1 5.6 %collective-permute-start.18 = (bf16[10,1,128]{2,1,0:T(2,128)(2,1)S(1)}, bf16[10,1,128]{2,1,0:T(2,128)(2,1)S(1)}, u32[]{:S(2)}, u32[]{:S(2)}) collective-permute-start(bf16[10,1,128]{2,1,0:T(2,128)(2,1)S(1)} %get-tuple-element.69), channel_id=1, source_target_pairs={{1,0},{2,1},{3,2},{4,3},{5,4},{6,5},{7,6},{8,7},{9,8},{10,9},{11,1... | collective-permute-start | bytes 7688 | tf_op jit(solution)/shard_map/ppermute | solution.py:20
  126.8 3.9 %collective-permute-start.20 = (bf16[8,128,512]{2,1,0:T(8,128)(2,1)}, bf16[8,128,512]{2,1,0:T(8,128)(2,1)}, u32[]{:S(2)}, u32[]{:S(2)}) collective-permute-start(bf16[8,128,512]{2,1,0:T(8,128)(2,1)} %multiply_convert_fusion.5), channel_id=1, source_target_pairs={{0,128},{1,129},{2,130},{3,131},{4,132},{5,133},{6,134},{7,135},{8... | collective-permute-start | bytes 3145736 | tf_op jit(solution)/shard_map/ppermute | solution.py:30
  132.0 16.9 %copy-start.13 = (bf16[8,128,512]{2,1,0:T(8,128)(2,1)}, bf16[8,128,512]{2,1,0:T(8,128)(2,1)S(1)}, u32[]{:S(2)}) copy-start(bf16[8,128,512]{2,1,0:T(8,128)(2,1)S(1)} %bitcast_select_fusion.2) | copy-start | bytes 3145732
  132.6 3.6 %collective-permute-start.21 = (bf16[1,128,128]{2,1,0:T(8,128)(2,1)S(1)}, bf16[1,128,128]{2,1,0:T(8,128)(2,1)S(1)}, u32[]{:S(2)}, u32[]{:S(2)}) collective-permute-start(bf16[1,128,128]{2,1,0:T(8,128)(2,1)S(1)} %get-tuple-element.92), channel_id=1, source_target_pairs={{0,32},{32,64},{64,96},{1,33},{33,65},{65,97},{2,34},{34,66},{66,9... | collective-permute-start | bytes 98312 | tf_op jit(solution)/shard_map/ppermute | solution.py:18
  134.6 5.8 %collective-permute-start.22 = (bf16[1,128,128]{2,1,0:T(8,128)(2,1)S(1)}, bf16[1,128,128]{2,1,0:T(8,128)(2,1)S(1)}, u32[]{:S(2)}, u32[]{:S(2)}) collective-permute-start(bf16[1,128,128]{2,1,0:T(8,128)(2,1)S(1)} %get-tuple-element.93), channel_id=1, source_target_pairs={{32,0},{64,32},{96,64},{33,1},{65,33},{97,65},{34,2},{66,34},{98,6... | collective-permute-start | bytes 98312 | tf_op jit(solution)/shard_map/ppermute | solution.py:20
  140.4 8.5 %collective-permute-start.23 = (bf16[10,1,128]{2,1,0:T(2,128)(2,1)S(1)}, bf16[10,1,128]{2,1,0:T(2,128)(2,1)S(1)}, u32[]{:S(2)}, u32[]{:S(2)}) collective-permute-start(bf16[10,1,128]{2,1,0:T(2,128)(2,1)S(1)} %get-tuple-element.64), channel_id=1, source_target_pairs={{0,1},{1,2},{2,3},{3,4},{4,5},{5,6},{6,7},{7,8},{8,9},{9,10},{10,1... | collective-permute-start | bytes 7688 | tf_op jit(solution)/shard_map/ppermute | solution.py:18
  143.5 6.5 %collective-permute-start.24 = (bf16[10,1,128]{2,1,0:T(2,128)(2,1)S(1)}, bf16[10,1,128]{2,1,0:T(2,128)(2,1)S(1)}, u32[]{:S(2)}, u32[]{:S(2)}) collective-permute-start(bf16[10,1,128]{2,1,0:T(2,128)(2,1)S(1)} %get-tuple-element.65), channel_id=1, source_target_pairs={{1,0},{2,1},{3,2},{4,3},{5,4},{6,5},{7,6},{8,7},{9,8},{10,9},{11,1... | collective-permute-start | bytes 7688 | tf_op jit(solution)/shard_map/ppermute | solution.py:20
  159.1 3.9 %collective-permute-start.25 = (bf16[8,128,512]{2,1,0:T(8,128)(2,1)}, bf16[8,128,512]{2,1,0:T(8,128)(2,1)}, u32[]{:S(2)}, u32[]{:S(2)}) collective-permute-start(bf16[8,128,512]{2,1,0:T(8,128)(2,1)} %multiply_convert_fusion.3), channel_id=1, source_target_pairs={{0,128},{1,129},{2,130},{3,131},{4,132},{5,133},{6,134},{7,135},{8... | collective-permute-start | bytes 3145736 | tf_op jit(solution)/shard_map/ppermute | solution.py:30
  164.3 5.2 %copy-start.8 = (bf16[8,128,512]{2,1,0:T(8,128)(2,1)}, bf16[8,128,512]{2,1,0:T(8,128)(2,1)S(1)}, u32[]{:S(2)}) copy-start(bf16[8,128,512]{2,1,0:T(8,128)(2,1)S(1)} %bitcast_select_fusion.1) | copy-start | bytes 3145732
  164.9 4.6 %collective-permute-start.26 = (bf16[1,128,128]{2,1,0:T(8,128)(2,1)S(1)}, bf16[1,128,128]{2,1,0:T(8,128)(2,1)S(1)}, u32[]{:S(2)}, u32[]{:S(2)}) collective-permute-start(bf16[1,128,128]{2,1,0:T(8,128)(2,1)S(1)} %get-tuple-element.88), channel_id=1, source_target_pairs={{0,32},{32,64},{64,96},{1,33},{33,65},{65,97},{2,34},{34,66},{66,9... | collective-permute-start | bytes 98312 | tf_op jit(solution)/shard_map/ppermute | solution.py:18
  166.9 5.8 %collective-permute-start.27 = (bf16[1,128,128]{2,1,0:T(8,128)(2,1)S(1)}, bf16[1,128,128]{2,1,0:T(8,128)(2,1)S(1)}, u32[]{:S(2)}, u32[]{:S(2)}) collective-permute-start(bf16[1,128,128]{2,1,0:T(8,128)(2,1)S(1)} %get-tuple-element.89), channel_id=1, source_target_pairs={{32,0},{64,32},{96,64},{33,1},{65,33},{97,65},{34,2},{66,34},{98,6... | collective-permute-start | bytes 98312 | tf_op jit(solution)/shard_map/ppermute | solution.py:20
  172.8 8.5 %collective-permute-start.28 = (bf16[10,1,128]{2,1,0:T(2,128)(2,1)S(1)}, bf16[10,1,128]{2,1,0:T(2,128)(2,1)S(1)}, u32[]{:S(2)}, u32[]{:S(2)}) collective-permute-start(bf16[10,1,128]{2,1,0:T(2,128)(2,1)S(1)} %get-tuple-element.60), channel_id=1, source_target_pairs={{0,1},{1,2},{2,3},{3,4},{4,5},{5,6},{6,7},{7,8},{8,9},{9,10},{10,1... | collective-permute-start | bytes 7688 | tf_op jit(solution)/shard_map/ppermute | solution.py:18
  174.9 7.4 %collective-permute-start.29 = (bf16[10,1,128]{2,1,0:T(2,128)(2,1)S(1)}, bf16[10,1,128]{2,1,0:T(2,128)(2,1)S(1)}, u32[]{:S(2)}, u32[]{:S(2)}) collective-permute-start(bf16[10,1,128]{2,1,0:T(2,128)(2,1)S(1)} %get-tuple-element.61), channel_id=1, source_target_pairs={{1,0},{2,1},{3,2},{4,3},{5,4},{6,5},{7,6},{8,7},{9,8},{10,9},{11,1... | collective-permute-start | bytes 7688 | tf_op jit(solution)/shard_map/ppermute | solution.py:20
  186.8 3.6 %copy-start.1 = (f32[1024,512]{1,0:T(8,128)S(1)}, f32[1024,512]{1,0:T(8,128)}, u32[]{:S(2)}) copy-start(f32[1024,512]{1,0:T(8,128)} %add_maximum_fusion.4) | copy-start | bytes 6291460
  188.9 7.8 %collective-permute-start.30 = (bf16[8,128,512]{2,1,0:T(8,128)(2,1)S(1)}, bf16[8,128,512]{2,1,0:T(8,128)(2,1)S(1)}, u32[]{:S(2)}, u32[]{:S(2)}) collective-permute-start(bf16[8,128,512]{2,1,0:T(8,128)(2,1)S(1)} %multiply_convert_fusion.1), channel_id=1, source_target_pairs={{0,128},{1,129},{2,130},{3,131},{4,132},{5,133},{6,134},{7,135},{8... | collective-permute-start | bytes 3145736 | tf_op jit(solution)/shard_map/ppermute | solution.py:30
  193.9 28.7 %collective-permute-start.19 = (bf16[3,8,128,512]{3,2,1,0:T(8,128)(2,1)}, bf16[3,8,128,512]{3,2,1,0:T(8,128)(2,1)}, u32[]{:S(2)}, u32[]{:S(2)}) collective-permute-start(bf16[3,8,128,512]{3,2,1,0:T(8,128)(2,1)} %pad_maximum_fusion), channel_id=1, source_target_pairs={{128,0},{129,1},{130,2},{131,3},{132,4},{133,5},{134,6},{135,7},{1... | collective-permute-start | bytes 9437192 | tf_op jit(solution)/shard_map/ppermute | solution.py:30
  198.0 5.4 %copy-start.6 = (bf16[8,128,512]{2,1,0:T(8,128)(2,1)}, bf16[8,128,512]{2,1,0:T(8,128)(2,1)S(1)}, u32[]{:S(2)}) copy-start(bf16[8,128,512]{2,1,0:T(8,128)(2,1)S(1)} %bitcast_select_fusion) | copy-start | bytes 3145732
  198.0 4.0 %copy-start.4 = (f32[1024,512]{1,0:T(8,128)S(1)}, f32[1024,512]{1,0:T(8,128)}, u32[]{:S(2)}) copy-start(f32[1024,512]{1,0:T(8,128)} %add_maximum_fusion.1) | copy-start | bytes 6291460
  198.6 4.8 %collective-permute-start.31 = (bf16[1,128,128]{2,1,0:T(8,128)(2,1)S(1)}, bf16[1,128,128]{2,1,0:T(8,128)(2,1)S(1)}, u32[]{:S(2)}, u32[]{:S(2)}) collective-permute-start(bf16[1,128,128]{2,1,0:T(8,128)(2,1)S(1)} %get-tuple-element.84), channel_id=1, source_target_pairs={{0,32},{32,64},{64,96},{1,33},{33,65},{65,97},{2,34},{34,66},{66,9... | collective-permute-start | bytes 98312 | tf_op jit(solution)/shard_map/ppermute | solution.py:18
  200.7 5.8 %collective-permute-start.32 = (bf16[1,128,128]{2,1,0:T(8,128)(2,1)S(1)}, bf16[1,128,128]{2,1,0:T(8,128)(2,1)S(1)}, u32[]{:S(2)}, u32[]{:S(2)}) collective-permute-start(bf16[1,128,128]{2,1,0:T(8,128)(2,1)S(1)} %get-tuple-element.85), channel_id=1, source_target_pairs={{32,0},{64,32},{96,64},{33,1},{65,33},{97,65},{34,2},{66,34},{98,6... | collective-permute-start | bytes 98312 | tf_op jit(solution)/shard_map/ppermute | solution.py:20
  206.5 8.7 %collective-permute-start.33 = (bf16[10,1,128]{2,1,0:T(2,128)(2,1)S(1)}, bf16[10,1,128]{2,1,0:T(2,128)(2,1)S(1)}, u32[]{:S(2)}, u32[]{:S(2)}) collective-permute-start(bf16[10,1,128]{2,1,0:T(2,128)(2,1)S(1)} %get-tuple-element.56), channel_id=1, source_target_pairs={{0,1},{1,2},{2,3},{3,4},{4,5},{5,6},{6,7},{7,8},{8,9},{9,10},{10,1... | collective-permute-start | bytes 7688 | tf_op jit(solution)/shard_map/ppermute | solution.py:18
  208.5 7.6 %collective-permute-start.34 = (bf16[10,1,128]{2,1,0:T(2,128)(2,1)S(1)}, bf16[10,1,128]{2,1,0:T(2,128)(2,1)S(1)}, u32[]{:S(2)}, u32[]{:S(2)}) collective-permute-start(bf16[10,1,128]{2,1,0:T(2,128)(2,1)S(1)} %get-tuple-element.57), channel_id=1, source_target_pairs={{1,0},{2,1},{3,2},{4,3},{5,4},{6,5},{7,6},{8,7},{9,8},{10,9},{11,1... | collective-permute-start | bytes 7688 | tf_op jit(solution)/shard_map/ppermute | solution.py:20
  (9 other events, 20.2 us)
where the time goes:
time: 228 us; the launch traced here: 226 us
  starting transfers between devices  99.8 us (44%)
  waiting for transfers between devices  43.5 us (19%)
  other arithmetic  39.4 us (17%)
  matrix products  36.6 us (16%)
  local copies, waits for them, and re-layouts  5.32 us (2%)
    ppermute x14, starting transfers between devices, extended(): lax.ppermute(head, axis, [((i + 1) % count, i) for i in range(ends)])  47.6 us
    ppermute x14, starting transfers between devices, extended(): lax.ppermute(tail, axis, [(i, (i + 1) % count) for i in range(ends)])  38.9 us
    ppermute x14, waiting for transfers between devices, extended(): lax.ppermute(head, axis, [((i + 1) % count, i) for i in range(ends)])  34.4 us
    convert_element_type x12, other arithmetic, run_block(): return z.astype(jnp.bfloat16)  20.8 us
    dot_general x7, matrix products, run_block(): z = jnp.dot(spatial, w_exp, preferred_element_type=jnp.float32)  17.9 us
    dot_general x56, matrix products, run_block(): jnp.dot(window, w_spa[dy, dx], preferred_element_type=jnp.float32)  15.7 us
    ppermute x7, starting transfers between devices, from_behind(): lax.ppermute(value, axis, [(source, source + steps) for source in range(i...  13.2 us
    select_n x7, other arithmetic, shards(): current = jnp.where(first, images[source], received)  9.35 us
  transfers between devices with their start and end apart: 35, of which 24 were waited for; matrix products, arithmetic and copies ran while one was open for 8% of the time, Pallas kernels for 0%

commit v1 on v0

v1 whole, which is shorter than its diff:
```python
import functools

import jax
import jax.numpy as jnp
from jax import lax
from jax.experimental import pallas as pl
from jax.experimental.pallas import tpu as pltpu
from jax.sharding import PartitionSpec as P

MESH = pl.DeviceIdType.MESH
TW = 64
F32 = jnp.float32
BF16 = jnp.bfloat16


def widen(row, times):
    return jnp.concatenate([row] * times, axis=1)


def blocks_kernel(
    grid,
    images,
    tissue_list,
    tissue_count,
    w_reduce,
    w_spatial,
    w_expand,
    inner_gain,
    inner_bias,
    outer_gain,
    outer_bias,
    h_out,
    spat_out,
    we_out,
    epi_out,
    img,
    wr,
    ws,
    wa,
    wb,
    we,
    gb,
    mk,
    rb,
    row_send,
    row_recv,
    edge_send,
    edge_recv,
    img_sem,
    w_sem,
    w_send_sem,
    w_recv_sem,
    row_send_sem,
    row_recv_sem,
    edge_send_sem,
    edge_recv_sem,
):
    n_row, n_col = grid
    slides, pairs, _, cols, chans = img.shape
    inner = wr.shape[2]
    last = cols - 1
    seg = lax.axis_index("segment")
    row = lax.axis_index("row")
    col = lax.axis_index("col")
    peer = {"segment": 1 - seg}
    up = lax.rem(row + n_row - 1, n_row)
    down = lax.rem(row + 1, n_row)
    left = lax.rem(col + n_col - 1, n_col)
    right = lax.rem(col + 1, n_col)
    beside = [
        {"row": r, "col": c} for c in (left, right) for r in (row, up, down)
    ]

    barrier = pltpu.get_barrier_semaphore()
    for other in [peer, {"row": up}, {"row": down}] + beside:
        pl.semaphore_signal(barrier, inc=1, device_id=other, device_id_type=MESH)

    loads = []
    for s in range(slides):
        load = pltpu.make_async_copy(
            images.at[seg * slides + s], img.at[s], img_sem.at[s]
        )
        if s == 0:
            load.start()
        loads.append(load)
    own = [
        pltpu.make_async_copy(w_reduce.at[0], wr.at[seg], w_sem.at[0]),
        pltpu.make_async_copy(w_spatial.at[0], ws.at[seg], w_sem.at[1]),
        pltpu.make_async_copy(w_expand.at[0], we.at[seg], w_sem.at[2]),
    ]
    for load in own:
        load.start()
    for load in loads[1:]:
        load.start()

    lines = [inner_gain[0].astype(F32), inner_bias[0].astype(F32)]
    for whole in (outer_gain[...].astype(F32), outer_bias[...].astype(F32)):
        lines += [whole[:, i * inner : (i + 1) * inner] for i in range(chans // inner)]
    lines.append(jnp.zeros((4, inner), F32))
    gb[seg] = jnp.concatenate(lines, axis=0)

    position = lax.broadcasted_iota(jnp.int32, (1, tissue_list.shape[1]), 1)
    for s in range(slides):
        slide = seg * slides + s
        listed = tissue_list[pl.ds(slide, 1), :]
        for t in range(cols // TW):
            tile = col * (cols // TW) + t
            hit = (listed == tile) & (position < tissue_count[slide])
            one = jnp.max(jnp.where(hit, 1.0, 0.0), axis=1, keepdims=True)
            mk[s, t] = jnp.broadcast_to(one, mk.shape[2:])

    pl.semaphore_wait(barrier, 9)

    def swap(src, dst, i):
        return pltpu.make_async_remote_copy(
            src_ref=src,
            dst_ref=dst.at[seg],
            send_sem=w_send_sem.at[i],
            recv_sem=w_recv_sem.at[i],
            device_id=peer,
            device_id_type=MESH,
        )

    swaps = [
        swap(w_reduce.at[0], wr, 0),
        swap(gb.at[seg], gb, 1),
        swap(w_spatial.at[0], ws, 2),
        swap(w_expand.at[0], we, 3),
    ]
    for copy in swaps:
        copy.start()

    def row_copies(e, s):
        for way, there in ((0, up), (1, down)):
            yield pltpu.make_async_remote_copy(
                src_ref=row_send.at[e, s, way],
                dst_ref=row_recv.at[e, s, 1 - way],
                send_sem=row_send_sem.at[e, s, way],
                recv_sem=row_recv_sem.at[e, s, 1 - way],
                device_id={"row": there},
                device_id_type=MESH,
            )

    def edge_copies(e, s):
        for i, there in enumerate(beside):
            side = i // 3
            slot = (1 - side) * 3 + (0, 2, 1)[i % 3]
            yield pltpu.make_async_remote_copy(
                src_ref=edge_send.at[e, s, side],
                dst_ref=edge_recv.at[e, s, slot],
                send_sem=edge_send_sem.at[e, s, i],
                recv_sem=edge_recv_sem.at[e, s, slot],
                device_id=there,
                device_id_type=MESH,
            )

    def store_shifted(e, s, half, red):
        place = rb.at[e, s, pl.ds(half, pairs), :, pl.ds((1 - half) * 3 * inner, 3 * inner)]
        place[...] = jnp.concatenate(
            [
                pltpu.roll(red, 1, 1).astype(BF16),
                red.astype(BF16),
                pltpu.roll(red, last, 1).astype(BF16),
            ],
            axis=2,
        )

    def reduce_half(e, s, half, x):
        v = jnp.dot(
            x.reshape(pairs * cols, chans), wr[e], preferred_element_type=F32
        ).reshape(pairs, cols // TW, TW, inner)
        mask = mk[s][:, 0:1]
        gain = (gb[e, 0:1] * mask)[None]
        bias = (gb[e, 2:3] * mask)[None]
        red = jnp.maximum(v * gain + bias, 0.0).reshape(pairs, cols, inner)
        if half == 0:
            row_send[e, s, 0] = red[0].astype(BF16)
        else:
            row_send[e, s, 1] = red[pairs - 1].astype(BF16)
        edge_send[e, s, 0, pl.ds(half * pairs, pairs)] = red[:, 0]
        edge_send[e, s, 1, pl.ds(half * pairs, pairs)] = red[:, last]
        return red

    def send(e, s):
        for copy in row_copies(e, s):
            copy.start()
        for copy in edge_copies(e, s):
            copy.start()

    def halo(e, s):
        for copy in row_copies(e, s):
            copy.wait_recv()
        for copy in edge_copies(e, s):
            copy.wait_recv()
        above, below = row > 0, row < n_row - 1
        at_left, at_right = col > 0, col < n_col - 1
        place = lax.broadcasted_iota(jnp.int32, (cols, inner), 0)
        spot = lax.broadcasted_iota(jnp.int32, (16, inner), 0)
        zero = jnp.zeros((1, inner), F32)

        def beyond(side, slot, line, there):
            pixel = edge_recv[e, s, 3 * side + slot, line : line + 1]
            return jnp.where(there & (at_right if side else at_left), pixel, zero)

        for way, there, slot, line, q, lane in (
            (0, above, 1, 2 * pairs - 1, 0, 0),
            (1, below, 2, 0, pairs, 3 * inner),
        ):
            got = jnp.where(there, row_recv[e, s, way].astype(F32), 0.0)
            before = jnp.where(place == 0, beyond(0, slot, line, there), pltpu.roll(got, 1, 0))
            after = jnp.where(place == last, beyond(1, slot, line, there), pltpu.roll(got, last, 0))
            rb[e, s, q, :, lane : lane + 3 * inner] = jnp.concatenate(
                [before.astype(BF16), got.astype(BF16), after.astype(BF16)], axis=1
            )
        for half in range(2):
            for p in range(pairs):
                line, lane = half * pairs + p, (1 - half) * 3 * inner
                here = rb.at[e, s, p + half, 0:16, lane : lane + inner]
                here[...] = jnp.where(
                    spot == 0, beyond(0, 0, line, True), here[...].astype(F32)
                ).astype(BF16)
                here = rb.at[e, s, p + half, cols - 16 : cols, lane + 2 * inner : lane + 3 * inner]
                here[...] = jnp.where(
                    spot == 15, beyond(1, 0, line, True), here[...].astype(F32)
                ).astype(BF16)

    def spatial(e, s):
        total = jnp.dot(
            rb[e, s, 0:pairs].reshape(pairs * cols, 6 * inner), wa[e], preferred_element_type=F32
        ) + jnp.dot(
            rb[e, s, 1 : pairs + 1].reshape(pairs * cols, 6 * inner),
            wb[e],
            preferred_element_type=F32,
        )
        gain, bias = widen(gb[e, 1:2], 2), widen(gb[e, 3:4], 2)
        return jnp.maximum(total * gain + bias, 0.0).astype(BF16)

    def spread(b):
        depth = 3 * inner
        zero = jnp.zeros((depth, inner), BF16)
        w = [ws[b, dy].reshape(depth, inner) for dy in range(3)]
        wa[b] = jnp.concatenate(
            [jnp.concatenate([w[0], zero], axis=1), jnp.concatenate([w[1], w[0]], axis=1)], axis=0
        )
        wb[b] = jnp.concatenate(
            [jnp.concatenate([w[2], w[1]], axis=1), jnp.concatenate([zero, w[2]], axis=1)], axis=0
        )

    def outer(b):
        n = chans // inner
        gain = jnp.concatenate([gb[b, 4 + i : 5 + i] for i in range(n)], axis=1)
        bias = jnp.concatenate([gb[b, 4 + n + i : 5 + n + i] for i in range(n)], axis=1)
        return gain, bias

    own[0].wait()
    for copy in swaps[:2]:
        copy.wait()

    def first_reduce(s, carry):
        pltpu.make_async_copy(images.at[seg * slides + s], img.at[s], img_sem.at[s]).wait()
        reds = [reduce_half(0, s, half, img[s, :, half]) for half in range(2)]
        send(0, s)
        for half in range(2):
            store_shifted(0, s, half, reds[half])
        return carry

    lax.fori_loop(0, slides, first_reduce, 0)

    for load in own[1:]:
        load.wait()
    for copy in swaps[2:]:
        copy.wait()
    spread(0)
    spread(1)

    def middle(s, carry):
        halo(0, s)
        sp = spatial(0, s)
        gain, bias = outer(0)
        mask = widen(mk[s][:, 0:1].reshape(cols // TW, inner), chans // inner)[:, None]
        reds = []
        for half in range(2):
            z = jnp.dot(
                sp[:, half * inner : (half + 1) * inner], we[0], preferred_element_type=F32
            ).reshape(pairs, cols, chans)
            z = z * gain + bias + img[s, :, half].astype(F32)
            z = jnp.maximum(z, 0.0).reshape(pairs, cols // TW, TW, chans) * mask[None]
            z = z.astype(BF16).reshape(pairs, cols, chans)
            h_out[s, :, half] = z
            reds.append(reduce_half(1, s, half, z))
        send(1, s)
        for half in range(2):
            store_shifted(1, s, half, reds[half])
        return carry

    lax.fori_loop(0, slides, middle, 0)

    def final(s, carry):
        halo(1, s)
        spat_out[s] = spatial(1, s).reshape(pairs, cols, 2 * inner)
        return carry

    we_out[...] = we[1]
    gain, bias = outer(1)
    for s in range(slides):
        for t in range(cols // TW):
            mask = widen(mk[s, t, 0:1], chans // inner)
            epi_out[s, t : t + 1] = gain * mask
            epi_out[s, 2 + t : 3 + t] = bias * mask
    lax.fori_loop(0, slides, final, 0)

    def drain(s, carry):
        for e in range(2):
            for copy in row_copies(e, s):
                copy.wait_send()
            for copy in edge_copies(e, s):
                copy.wait_send()
        return carry

    lax.fori_loop(0, slides, drain, 0)


def expand_kernel(h, spat, we, epi, out, held, sem):
    slides, pairs, _, cols, chans = h.shape
    inner = we.shape[0]
    tiles = cols // TW

    def one(s, carry):
        for half in range(2):
            z = jnp.dot(
                spat[s].reshape(pairs * cols, 2 * inner)[:, half * inner : (half + 1) * inner],
                we[...],
                preferred_element_type=F32,
            ).reshape(pairs, tiles, TW, chans)
            gain = epi[s, 0:tiles][None, :, None]
            bias = epi[s, 2 : 2 + tiles][None, :, None]
            z = z * gain + bias + h[s, :, half].astype(F32).reshape(pairs, tiles, TW, chans)
            held[s, :, half] = jnp.maximum(z, 0.0).astype(BF16).reshape(pairs, cols, chans)
        pltpu.make_async_copy(held.at[s], out.at[s], sem.at[s]).start()
        return carry

    lax.fori_loop(0, slides, one, 0)
    for s in range(slides):
        pltpu.make_async_copy(held.at[s], out.at[s], sem.at[s]).wait()


def shards(grid, images, tissue_list, tissue_count, *weights):
    total, rows, cols, chans = images.shape
    slides, pairs = total // 2, rows // 2
    inner = weights[0].shape[2]
    w_reduce, w_spatial, w_expand, inner_gain, inner_bias, outer_gain, outer_bias = weights
    w_spatial = w_spatial.reshape(1, 3, 3, inner, inner)
    hbm = pl.BlockSpec(memory_space=pltpu.HBM)
    vmem = pl.BlockSpec(memory_space=pltpu.VMEM)
    smem = pl.BlockSpec(memory_space=pltpu.SMEM)
    dma = pltpu.SemaphoreType.DMA
    h, spat, we, epi = pl.pallas_call(
        functools.partial(blocks_kernel, grid),
        out_shape=(
            pltpu.VMEM((slides, pairs, 2, cols, chans), BF16),
            pltpu.VMEM((slides, pairs, cols, 2 * inner), BF16),
            pltpu.VMEM((inner, chans), BF16),
            pltpu.VMEM((slides, 4, chans), F32),
        ),
        in_specs=[hbm, vmem, smem, hbm, hbm, hbm] + [vmem] * 4,
        out_specs=(vmem,) * 4,
        scratch_shapes=[
            pltpu.VMEM((slides, pairs, 2, cols, chans), BF16),
            pltpu.VMEM((2, chans, inner), BF16),
            pltpu.VMEM((2, 3, 3, inner, inner), BF16),
            pltpu.VMEM((2, 6 * inner, 2 * inner), BF16),
            pltpu.VMEM((2, 6 * inner, 2 * inner), BF16),
            pltpu.VMEM((2, inner, chans), BF16),
            pltpu.VMEM((2, 16, inner), F32),
            pltpu.VMEM((slides, cols // TW, 8, inner), F32),
            pltpu.VMEM((2, slides, pairs + 1, cols, 6 * inner), BF16),
            pltpu.VMEM((2, slides, 2, cols, inner), BF16),
            pltpu.VMEM((2, slides, 2, cols, inner), BF16),
            pltpu.VMEM((2, slides, 2, rows, inner), F32),
            pltpu.VMEM((2, slides, 6, rows, inner), F32),
            dma((slides,)),
            dma((3,)),
            dma((4,)),
            dma((4,)),
            dma((2, slides, 2)),
            dma((2, slides, 2)),
            dma((2, slides, 6)),
            dma((2, slides, 6)),
        ],
        compiler_params=pltpu.CompilerParams(
            collective_id=0, has_side_effects=True, vmem_limit_bytes=40 * 2**20
        ),
        name="blocks",
    )(
        images.reshape(total, pairs, 2, cols, chans),
        tissue_list,
        tissue_count,
        w_reduce,
        w_spatial,
        w_expand,
        inner_gain,
        inner_bias,
        outer_gain,
        outer_bias,
    )
    out = pl.pallas_call(
        expand_kernel,
        out_shape=jax.ShapeDtypeStruct((slides, pairs, 2, cols, chans), BF16),
        in_specs=[vmem] * 4,
        out_specs=hbm,
        scratch_shapes=[
            pltpu.VMEM((slides, pairs, 2, cols, chans), BF16),
            dma((slides,)),
        ],
        compiler_params=pltpu.CompilerParams(vmem_limit_bytes=24 * 2**20),
        name="expand",
    )(h, spat, we, epi)
    return out.reshape(slides, rows, cols, chans)


def solution(mesh):
    placed = (
        P(None, "row", "col", None),
        P(),
        P(),
        P("segment", None, None),
        P("segment", None, None, None, None),
        P("segment", None, None),
        P("segment", None, None),
        P("segment", None, None),
        P("segment", None),
        P("segment", None),
    )
    return jax.shard_map(
        functools.partial(shards, (mesh.shape["row"], mesh.shape["col"])),
        mesh=mesh,
        in_specs=placed,
        out_specs=P("segment", "row", "col", None),
        check_vma=False,
    )
```

time: 228 us -> 43.2 us (0.19)
  the two profiles are of different devices: /device:TPU:24 before, /device:TPU:1 now
where the time goes in v1:
time: 43.2 us; the launch traced here: 42.9 us
  Pallas kernels  33.3 us (77%)
  local copies, waits for them, and re-layouts  9.57 us (22%)
    pallas_call x1, Pallas kernels, shards(): pl.pallas_call(functools.partial(blocks_kernel, grid), out_shape=(pltpu.V...  30.7 us
    unnamed x20, local copies, waits for them, and re-layouts  9.57 us
    pallas_call x1, Pallas kernels, shards(): pl.pallas_call(expand_kernel, out_shape=jax.ShapeDtypeStruct((slides, pai...  2.59 us

profile of v1, /device:TPU:1, one launch (start us, length us, event | category | flops | bytes accessed | tf_op | source)
XLA Modules:
  0.0 42.9 jit_solution(6052523910384117122)
XLA Ops:
  0.0 0.0 copy-start
  0.0 2.8 %copy-done = bf16[6,8,128,512]{3,2,1,0:T(8,128)(2,1)S(1)} copy-done((bf16[6,8,128,512]{3,2,1,0:T(8,128)(2,1)S(1)}, bf16[6,8,128,512]{3,2,1,0:T(8,128)(2,1)}, u32[]{:S(2)}) %copy-start) | copy-done | bytes 6291480
  2.8 0.0 copy-start.1
  2.8 1.0 %copy-done.1 = bf16[1,3,3,128,128]{4,3,2,1,0:T(8,128)(2,1)S(1)} copy-done((bf16[1,3,3,128,128]{4,3,2,1,0:T(8,128)(2,1)S(1)}, bf16[1,3,3,128,128]{4,3,2,1,0:T(8,128)(2,1)}, u32[]{:S(2)}) %copy-start.1) | copy-done | bytes 294936
  3.7 0.0 copy-start.2
  3.8 0.9 %copy-done.2 = bf16[1,512,128]{2,1,0:T(8,128)(2,1)S(1)} copy-done((bf16[1,512,128]{2,1,0:T(8,128)(2,1)S(1)}, bf16[1,512,128]{2,1,0:T(8,128)(2,1)}, u32[]{:S(2)}) %copy-start.2) | copy-done | bytes 131096
  4.7 0.0 copy-start.3
  4.7 0.9 %copy-done.3 = bf16[1,128,512]{2,1,0:T(8,128)(2,1)S(1)} copy-done((bf16[1,128,512]{2,1,0:T(8,128)(2,1)S(1)}, bf16[1,128,512]{2,1,0:T(8,128)(2,1)}, u32[]{:S(2)}) %copy-start.3) | copy-done | bytes 131096
  5.6 0.0 copy-start.4
  5.6 0.7 %copy-done.4 = s32[6,64]{1,0:T(8,128)S(1)} copy-done((s32[6,64]{1,0:T(8,128)S(1)}, s32[6,64]{1,0:T(8,128)}, u32[]{:S(2)}) %copy-start.4) | copy-done | bytes 1560
  6.2 0.0 copy-start.5
  6.2 0.7 %copy-done.5 = bf16[1,512]{1,0:T(2,128)(2,1)S(1)} copy-done((bf16[1,512]{1,0:T(2,128)(2,1)S(1)}, bf16[1,512]{1,0:T(2,128)(2,1)}, u32[]{:S(2)}) %copy-start.5) | copy-done | bytes 1048
  6.9 0.0 copy-start.6
  6.9 0.7 %copy-done.6 = bf16[1,512]{1,0:T(2,128)(2,1)S(1)} copy-done((bf16[1,512]{1,0:T(2,128)(2,1)S(1)}, bf16[1,512]{1,0:T(2,128)(2,1)}, u32[]{:S(2)}) %copy-start.6) | copy-done | bytes 1048
  7.6 0.0 copy-start.7
  7.6 0.7 %copy-done.7 = s32[6]{0:T(128)S(1)} copy-done((s32[6]{0:T(128)S(1)}, s32[6]{0:T(128)}, u32[]{:S(2)}) %copy-start.7) | copy-done | bytes 48
  8.3 0.0 copy-start.8
  8.3 0.7 %copy-done.8 = bf16[1,2,128]{2,1,0:T(2,128)(2,1)S(1)} copy-done((bf16[1,2,128]{2,1,0:T(2,128)(2,1)S(1)}, bf16[1,2,128]{2,1,0:T(2,128)(2,1)}, u32[]{:S(2)}) %copy-start.8) | copy-done | bytes 536
  8.9 0.0 copy-start.9
  8.9 0.7 %copy-done.9 = bf16[1,2,128]{2,1,0:T(2,128)(2,1)S(1)} copy-done((bf16[1,2,128]{2,1,0:T(2,128)(2,1)S(1)}, bf16[1,2,128]{2,1,0:T(2,128)(2,1)}, u32[]{:S(2)}) %copy-start.9) | copy-done | bytes 536
  9.6 30.7 %blocks.1 = (bf16[3,4,2,128,512]{4,3,2,1,0:T(8,128)(2,1)S(1)}, bf16[3,4,128,256]{3,2,1,0:T(8,128)(2,1)S(1)}, bf16[128,512]{1,0:T(8,128)(2,1)S(1)}, f32[3,4,512]{2,1,0:T(4,128)S(1)}) custom-call(bf16[6,4,2,128,512]{4,3,2,1,0:T(8,128)(2,1)S(1)} %bitcast.2, s32[6,64]{1,0:T(8,128)S(1)} %copy-done.4, s32[6]{0:T(128)S(1)} %copy-done.7, ...), custom_call_target="tpu_custom_call" | custom-call | tf_op jit(solution)/shard_map/blocks/pallas_call | solution.py:357
  40.3 2.6 %expand.1 = bf16[3,4,2,128,512]{4,3,2,1,0:T(8,128)(2,1)} custom-call(bf16[3,4,2,128,512]{4,3,2,1,0:T(8,128)(2,1)S(1)} %get-tuple-element.9.h, bf16[3,4,128,256]{3,2,1,0:T(8,128)(2,1)S(1)} %get-tuple-element.10.spat, bf16[128,512]{1,0:T(8,128)(2,1)S(1)} %get-tuple-element.11.we, f32[3,4,512]{2,1,0:T(4,128)S(1)} %get-tuple-element.12.epi), custom_call_target="tpu_custom_call" | custom-call | tf_op jit(solution)/shard_map/expand/pallas_call | solution.py:406
Async XLA Ops:
  0.0 2.8 %copy-start = (bf16[6,8,128,512]{3,2,1,0:T(8,128)(2,1)S(1)}, bf16[6,8,128,512]{3,2,1,0:T(8,128)(2,1)}, u32[]{:S(2)}) copy-start(bf16[6,8,128,512]{3,2,1,0:T(8,128)(2,1)} %param.10) | copy-start | bytes 18874372
  2.8 1.0 %copy-start.1 = (bf16[1,3,3,128,128]{4,3,2,1,0:T(8,128)(2,1)S(1)}, bf16[1,3,3,128,128]{4,3,2,1,0:T(8,128)(2,1)}, u32[]{:S(2)}) copy-start(bf16[1,3,3,128,128]{4,3,2,1,0:T(8,128)(2,1)} %w_spatial.1) | copy-start | bytes 884740
  3.7 0.9 %copy-start.2 = (bf16[1,512,128]{2,1,0:T(8,128)(2,1)S(1)}, bf16[1,512,128]{2,1,0:T(8,128)(2,1)}, u32[]{:S(2)}) copy-start(bf16[1,512,128]{2,1,0:T(8,128)(2,1)} %w_reduce.1) | copy-start | bytes 393220
  4.7 0.9 %copy-start.3 = (bf16[1,128,512]{2,1,0:T(8,128)(2,1)S(1)}, bf16[1,128,512]{2,1,0:T(8,128)(2,1)}, u32[]{:S(2)}) copy-start(bf16[1,128,512]{2,1,0:T(8,128)(2,1)} %w_expand.1) | copy-start | bytes 393220
  5.6 0.7 %copy-start.4 = (s32[6,64]{1,0:T(8,128)S(1)}, s32[6,64]{1,0:T(8,128)}, u32[]{:S(2)}) copy-start(s32[6,64]{1,0:T(8,128)} %tissue_list.1) | copy-start | bytes 4612
  6.2 0.7 %copy-start.5 = (bf16[1,512]{1,0:T(2,128)(2,1)S(1)}, bf16[1,512]{1,0:T(2,128)(2,1)}, u32[]{:S(2)}) copy-start(bf16[1,512]{1,0:T(2,128)(2,1)} %outer_gain.1) | copy-start | bytes 3076
  6.9 0.7 %copy-start.6 = (bf16[1,512]{1,0:T(2,128)(2,1)S(1)}, bf16[1,512]{1,0:T(2,128)(2,1)}, u32[]{:S(2)}) copy-start(bf16[1,512]{1,0:T(2,128)(2,1)} %outer_bias.1) | copy-start | bytes 3076
  7.6 0.7 %copy-start.7 = (s32[6]{0:T(128)S(1)}, s32[6]{0:T(128)}, u32[]{:S(2)}) copy-start(s32[6]{0:T(128)} %tissue_count.1) | copy-start | bytes 76
  8.3 0.7 %copy-start.8 = (bf16[1,2,128]{2,1,0:T(2,128)(2,1)S(1)}, bf16[1,2,128]{2,1,0:T(2,128)(2,1)}, u32[]{:S(2)}) copy-start(bf16[1,2,128]{2,1,0:T(2,128)(2,1)} %inner_gain.1) | copy-start | bytes 1540
  8.9 0.7 %copy-start.9 = (bf16[1,2,128]{2,1,0:T(2,128)(2,1)S(1)}, bf16[1,2,128]{2,1,0:T(2,128)(2,1)}, u32[]{:S(2)}) copy-start(bf16[1,2,128]{2,1,0:T(2,128)(2,1)} %inner_bias.1) | copy-start | bytes 1540

commit v2 on v1

--- a/solution.py
+++ b/solution.py
@@ -11,10 +11,15 @@
 TW = 64
 F32 = jnp.float32
 BF16 = jnp.bfloat16
+remote = pltpu.make_async_remote_copy
 
 
 def widen(row, times):
     return jnp.concatenate([row] * times, axis=1)
+
+
+def inside(i, n):
+    return (i >= 0) & (i < n)
 
 
 def blocks_kernel(
@@ -34,6 +39,12 @@
     we_out,
     epi_out,
     img,
+    listed,
+    counts,
+    ig,
+    ib,
+    og,
+    ob,
     wr,
     ws,
     wa,
@@ -50,10 +61,8 @@
     w_sem,
     w_send_sem,
     w_recv_sem,
-    row_send_sem,
-    row_recv_sem,
-    edge_send_sem,
-    edge_recv_sem,
+    send_sem,
+    recv_sem,
 ):
     n_row, n_col = grid
     slides, pairs, _, cols, chans = img.shape
@@ -63,56 +72,76 @@
     row = lax.axis_index("row")
     col = lax.axis_index("col")
     peer = {"segment": 1 - seg}
-    up = lax.rem(row + n_row - 1, n_row)
-    down = lax.rem(row + 1, n_row)
-    left = lax.rem(col + n_col - 1, n_col)
-    right = lax.rem(col + 1, n_col)
-    beside = [
-        {"row": r, "col": c} for c in (left, right) for r in (row, up, down)
+    around = [
+        (i, j, inside(row + i, n_row) & inside(col + j, n_col))
+        for j in (0, -1, 1)
+        for i in (-1, 1, 0)
+        if i or j
     ]
 
+    def at(i, j):
+        return {"row": row + i, "col": col + j}
+
     barrier = pltpu.get_barrier_semaphore()
-    for other in [peer, {"row": up}, {"row": down}] + beside:
+
+    def greet(other):
         pl.semaphore_signal(barrier, inc=1, device_id=other, device_id_type=MESH)
 
-    loads = []
+    greet(peer)
+    for i, j, there in around:
+        pl.when(there)(functools.partial(greet, at(i, j)))
+
+    def image_load(s):
+        return pltpu.make_async_copy(images.at[seg * slides + s], img.at[s], img_sem.at[s])
+
+    own = [
+        pltpu.make_async_copy(src, dst, w_sem.at[i])
+        for i, (src, dst) in enumerate(
+            (
+                (w_reduce.at[0], wr.at[seg]),
+                (w_spatial.at[0], ws.at[seg]),
+                (w_expand.at[0], we.at[seg]),
+                (inner_gain, ig),
+                (inner_bias, ib),
+                (outer_gain, og),
+                (outer_bias, ob),
+                (tissue_count, counts),
+                (tissue_list, listed),
+            )
+        )
+    ]
+    for load in own[3:] + own[:1]:
+        load.start()
     for s in range(slides):
-        load = pltpu.make_async_copy(
-            images.at[seg * slides + s], img.at[s], img_sem.at[s]
-        )
-        if s == 0:
-            load.start()
-        loads.append(load)
-    own = [
-        pltpu.make_async_copy(w_reduce.at[0], wr.at[seg], w_sem.at[0]),
-        pltpu.make_async_copy(w_spatial.at[0], ws.at[seg], w_sem.at[1]),
-        pltpu.make_async_copy(w_expand.at[0], we.at[seg], w_sem.at[2]),
-    ]
-    for load in own:
+        image_load(s).start()
+    for load in own[1:3]:
         load.start()
-    for load in loads[1:]:
-        load.start()
-
-    lines = [inner_gain[0].astype(F32), inner_bias[0].astype(F32)]
-    for whole in (outer_gain[...].astype(F32), outer_bias[...].astype(F32)):
+    for load in own[3:]:
+        load.wait()
+
+    lines = [ig[0].astype(F32), ib[0].astype(F32)]
+    for whole in (og[...].astype(F32), ob[...].astype(F32)):
         lines += [whole[:, i * inner : (i + 1) * inner] for i in range(chans // inner)]
     lines.append(jnp.zeros((4, inner), F32))
     gb[seg] = jnp.concatenate(lines, axis=0)
 
-    position = lax.broadcasted_iota(jnp.int32, (1, tissue_list.shape[1]), 1)
+    position = lax.broadcasted_iota(jnp.int32, (1, listed.shape[1]), 1)
     for s in range(slides):
         slide = seg * slides + s
-        listed = tissue_list[pl.ds(slide, 1), :]
+        here = listed[pl.ds(slide, 1), :]
         for t in range(cols // TW):
             tile = col * (cols // TW) + t
-            hit = (listed == tile) & (position < tissue_count[slide])
+            hit = (here == tile) & (position < counts[slide])
             one = jnp.max(jnp.where(hit, 1.0, 0.0), axis=1, keepdims=True)
             mk[s, t] = jnp.broadcast_to(one, mk.shape[2:])
 
-    pl.semaphore_wait(barrier, 9)
+    partners = 1
+    for _, _, there in around:
+        partners = partners + there.astype(jnp.int32)
+    pl.semaphore_wait(barrier, partners)
 
     def swap(src, dst, i):
-        return pltpu.make_async_remote_copy(
+        return remote(
             src_ref=src,
             dst_ref=dst.at[seg],
             send_sem=w_send_sem.at[i],
@@ -130,29 +159,25 @@
     for copy in swaps:
         copy.start()
 
-    def row_copies(e, s):
-        for way, there in ((0, up), (1, down)):
-            yield pltpu.make_async_remote_copy(
-                src_ref=row_send.at[e, s, way],
-                dst_ref=row_recv.at[e, s, 1 - way],
-                send_sem=row_send_sem.at[e, s, way],
-                recv_sem=row_recv_sem.at[e, s, 1 - way],
-                device_id={"row": there},
+    def sends(e, s):
+        for n, (i, j, there) in enumerate(around):
+            if j == 0:
+                src, dst = row_send.at[e, s, n], row_recv.at[e, s, 1 - n]
+            else:
+                src = edge_send.at[e, s, (1 + j) // 2]
+                dst = edge_recv.at[e, s, (1 - j) // 2 * 3 + (i + 2 if i == 0 else (1 - i) // 2)]
+            yield there, remote(
+                src_ref=src,
+                dst_ref=dst,
+                send_sem=send_sem.at[e, s, n],
+                recv_sem=recv_sem.at[e, s, mirror(n)],
+                device_id=at(i, j),
                 device_id_type=MESH,
             )
 
-    def edge_copies(e, s):
-        for i, there in enumerate(beside):
-            side = i // 3
-            slot = (1 - side) * 3 + (0, 2, 1)[i % 3]
-            yield pltpu.make_async_remote_copy(
-                src_ref=edge_send.at[e, s, side],
-                dst_ref=edge_recv.at[e, s, slot],
-                send_sem=edge_send_sem.at[e, s, i],
-                recv_sem=edge_recv_sem.at[e, s, slot],
-                device_id=there,
-                device_id_type=MESH,
-            )
+    def mirror(n):
+        i, j, _ = around[n]
+        return [(a, b) for a, b, _ in around].index((-i, -j))
 
     def store_shifted(e, s, half, red):
         place = rb.at[e, s, pl.ds(half, pairs), :, pl.ds((1 - half) * 3 * inner, 3 * inner)]
@@ -182,16 +207,13 @@
         return red
 
     def send(e, s):
-        for copy in row_copies(e, s):
-            copy.start()
-        for copy in edge_copies(e, s):
-            copy.start()
+        for there, copy in sends(e, s):
+            pl.when(there)(copy.start)
 
     def halo(e, s):
-        for copy in row_copies(e, s):
-            copy.wait_recv()
-        for copy in edge_copies(e, s):
-            copy.wait_recv()
+        copies = list(sends(e, s))
+        for n, (there, _) in enumerate(copies):
+            pl.when(there)(copies[mirror(n)][1].wait_recv)
         above, below = row > 0, row < n_row - 1
         at_left, at_right = col > 0, col < n_col - 1
         place = lax.broadcasted_iota(jnp.int32, (cols, inner), 0)
@@ -203,8 +225,8 @@
             return jnp.where(there & (at_right if side else at_left), pixel, zero)
 
         for way, there, slot, line, q, lane in (
-            (0, above, 1, 2 * pairs - 1, 0, 0),
-            (1, below, 2, 0, pairs, 3 * inner),
+            (0, above, 0, 2 * pairs - 1, 0, 0),
+            (1, below, 1, 0, pairs, 3 * inner),
         ):
             got = jnp.where(there, row_recv[e, s, way].astype(F32), 0.0)
             before = jnp.where(place == 0, beyond(0, slot, line, there), pltpu.roll(got, 1, 0))
@@ -217,11 +239,11 @@
                 line, lane = half * pairs + p, (1 - half) * 3 * inner
                 here = rb.at[e, s, p + half, 0:16, lane : lane + inner]
                 here[...] = jnp.where(
-                    spot == 0, beyond(0, 0, line, True), here[...].astype(F32)
+                    spot == 0, beyond(0, 2, line, True), here[...].astype(F32)
                 ).astype(BF16)
                 here = rb.at[e, s, p + half, cols - 16 : cols, lane + 2 * inner : lane + 3 * inner]
                 here[...] = jnp.where(
-                    spot == 15, beyond(1, 0, line, True), here[...].astype(F32)
+                    spot == 15, beyond(1, 2, line, True), here[...].astype(F32)
                 ).astype(BF16)
 
     def spatial(e, s):
@@ -257,7 +279,7 @@
         copy.wait()
 
     def first_reduce(s, carry):
-        pltpu.make_async_copy(images.at[seg * slides + s], img.at[s], img_sem.at[s]).wait()
+        image_load(s).wait()
         reds = [reduce_half(0, s, half, img[s, :, half]) for half in range(2)]
         send(0, s)
         for half in range(2):
@@ -266,7 +288,7 @@
 
     lax.fori_loop(0, slides, first_reduce, 0)
 
-    for load in own[1:]:
+    for load in own[1:3]:
         load.wait()
     for copy in swaps[2:]:
         copy.wait()
@@ -311,10 +333,8 @@
 
     def drain(s, carry):
         for e in range(2):
-            for copy in row_copies(e, s):
-                copy.wait_send()
-            for copy in edge_copies(e, s):
-                copy.wait_send()
+            for there, copy in sends(e, s):
+                pl.when(there)(copy.wait_send)
         return carry
 
     lax.fori_loop(0, slides, drain, 0)
@@ -352,7 +372,6 @@
     w_spatial = w_spatial.reshape(1, 3, 3, inner, inner)
     hbm = pl.BlockSpec(memory_space=pltpu.HBM)
     vmem = pl.BlockSpec(memory_space=pltpu.VMEM)
-    smem = pl.BlockSpec(memory_space=pltpu.SMEM)
     dma = pltpu.SemaphoreType.DMA
     h, spat, we, epi = pl.pallas_call(
         functools.partial(blocks_kernel, grid),
@@ -362,10 +381,16 @@
             pltpu.VMEM((inner, chans), BF16),
             pltpu.VMEM((slides, 4, chans), F32),
         ),
-        in_specs=[hbm, vmem, smem, hbm, hbm, hbm] + [vmem] * 4,
+        in_specs=[hbm] * 10,
         out_specs=(vmem,) * 4,
         scratch_shapes=[
             pltpu.VMEM((slides, pairs, 2, cols, chans), BF16),
+            pltpu.VMEM(tissue_list.shape, jnp.int32),
+            pltpu.SMEM(tissue_count.shape, jnp.int32),
+            pltpu.VMEM(inner_gain.shape, BF16),
+            pltpu.VMEM(inner_bias.shape, BF16),
+            pltpu.VMEM(outer_gain.shape, BF16),
+            pltpu.VMEM(outer_bias.shape, BF16),
             pltpu.VMEM((2, chans, inner), BF16),
             pltpu.VMEM((2, 3, 3, inner, inner), BF16),
             pltpu.VMEM((2, 6 * inner, 2 * inner), BF16),
@@ -379,29 +404,32 @@
             pltpu.VMEM((2, slides, 2, rows, inner), F32),
             pltpu.VMEM((2, slides, 6, rows, inner), F32),
             dma((slides,)),
-            dma((3,)),
+            dma((9,)),
             dma((4,)),
             dma((4,)),
-            dma((2, slides, 2)),
-            dma((2, slides, 2)),
-            dma((2, slides, 6)),
-            dma((2, slides, 6)),
+            dma((2, slides, 8)),
+            dma((2, slides, 8)),
         ],
         compiler_params=pltpu.CompilerParams(
             collective_id=0, has_side_effects=True, vmem_limit_bytes=40 * 2**20
         ),
         name="blocks",
     )(
-        images.reshape(total, pairs, 2, cols, chans),
-        tissue_list,
-        tissue_count,
-        w_reduce,
-        w_spatial,
-        w_expand,
-        inner_gain,
-        inner_bias,
-        outer_gain,
-        outer_bias,
+        *(
+            pltpu.with_memory_space_constraint(x, pltpu.HBM)
+            for x in (
+                images.reshape(total, pairs, 2, cols, chans),
+                tissue_list,
+                tissue_count,
+                w_reduce,
+                w_spatial,
+                w_expand,
+                inner_gain,
+                inner_bias,
+                outer_gain,
+                outer_bias,
+            )
+        )
     )
     out = pl.pallas_call(
         expand_kernel,

time: 43.2 us -> 27.9 us (0.65)
  the two profiles are of different devices: /device:TPU:1 before, /device:TPU:24 now
where the time goes in v2:
time: 27.9 us; the launch traced here: 27.8 us
  Pallas kernels  27.8 us (100%)
    pallas_call x1, Pallas kernels, shards(): pl.pallas_call(functools.partial(blocks_kernel, grid), out_shape=(pltpu.V...  25.3 us
    pallas_call x1, Pallas kernels, shards(): pl.pallas_call(expand_kernel, out_shape=jax.ShapeDtypeStruct((slides, pai...  2.57 us

profile of v2, /device:TPU:24, one launch (start us, length us, event | category | flops | bytes accessed | tf_op | source)
XLA Modules:
  0.0 27.8 jit_solution(18005445614629427804)
XLA Ops:
  0.0 25.3 %blocks.1 = (bf16[3,4,2,128,512]{4,3,2,1,0:T(8,128)(2,1)S(1)}, bf16[3,4,128,256]{3,2,1,0:T(8,128)(2,1)S(1)}, bf16[128,512]{1,0:T(8,128)(2,1)S(1)}, f32[3,4,512]{2,1,0:T(4,128)S(1)}) custom-call(bf16[6,4,2,128,512]{4,3,2,1,0:T(8,128)(2,1)} %bitcast.2, s32[6,64]{1,0:T(8,128)} %tissue_list.1, s32[6]{0:T(128)} %tissue_count.1, bf16[1,512,128]{2,1,0:T(8,128)(2,1)} %w_reduce.1, ...), custom_call_target="tpu_custom_call" | custom-call | tf_op jit(solution)/shard_map/blocks/pallas_call | solution.py:376
  25.3 2.6 %expand.1 = bf16[3,4,2,128,512]{4,3,2,1,0:T(8,128)(2,1)} custom-call(bf16[3,4,2,128,512]{4,3,2,1,0:T(8,128)(2,1)S(1)} %get-tuple-element.9.h, bf16[3,4,128,256]{3,2,1,0:T(8,128)(2,1)S(1)} %get-tuple-element.10.spat, bf16[128,512]{1,0:T(8,128)(2,1)S(1)} %get-tuple-element.11.we, f32[3,4,512]{2,1,0:T(4,128)S(1)} %get-tuple-element.12.epi), custom_call_target="tpu_custom_call" | custom-call | tf_op jit(solution)/shard_map/expand/pallas_call | solution.py:434

commit v3 on v2

--- a/solution.py
+++ b/solution.py
@@ -2,6 +2,8 @@
 
 import jax
 import jax.numpy as jnp
+import ml_dtypes
+import numpy as np
 from jax import lax
 from jax.experimental import pallas as pl
 from jax.experimental.pallas import tpu as pltpu
@@ -12,6 +14,51 @@
 F32 = jnp.float32
 BF16 = jnp.bfloat16
 remote = pltpu.make_async_remote_copy
+
+
+RUN = 8
+
+
+def selections(rows):
+    gather = np.zeros((2, 48, 128), np.float32)
+    window = np.zeros((2, 2, 96, 256), np.float32)
+    scatter = np.zeros((6, 128, 128), np.float32)
+    for side in range(2):
+        own = [12 * side + q for q in range(4)]
+        outer = own[2:] if side else own[:2]
+        for q in range(2):
+            for r in range(rows):
+                gather[side, q * 8 + r, r * 16 + outer[q]] = 1
+            for t in range(2):
+                gather[side, 32 + q * 2 + t, t * 16 + outer[q]] = 1
+                gather[side, 40 + q * 2 + t, (rows - 2 + t) * 16 + outer[q]] = 1
+        for q in range(4):
+            for t in range(2):
+                gather[side, 16 + q * 2 + t, t * 16 + own[q]] = 1
+                gather[side, 24 + q * 2 + t, (rows - 2 + t) * 16 + own[q]] = 1
+        for half in range(2):
+            to = window[side, half]
+            for q in range(4):
+                w = (q if side else q + 2) * 16
+                for r in range(rows):
+                    to[w + r, r * 16 + own[q]] = 1
+                for t in range(2):
+                    to[w + 8 + t, 160 + side * 8 + q * 2 + t] = 1
+                    to[w + 14 + t, 144 + side * 8 + q * 2 + t] = 1
+            for q in range(2):
+                w = (q + 4 if side else q) * 16
+                for r in range(rows):
+                    to[w + r, 128 + q * 8 + r] = 1
+                for t in range(2):
+                    to[w + 8 + t, 192 + half * 8 + q * 2 + t] = 1
+                    to[w + 14 + t, 176 + half * 8 + q * 2 + t] = 1
+        for s in range(3):
+            strip = s * 2 + side
+            for q in range(2):
+                for r in range(rows):
+                    scatter[strip, r * 16 + 14 * side + q, strip * 16 + q * 8 + r] = 1
+    window = window.reshape(4, 96, 256)
+    return [x.astype(ml_dtypes.bfloat16) for x in (gather, window, scatter)]
 
 
 def widen(row, times):
@@ -34,10 +81,14 @@
     inner_bias,
     outer_gain,
     outer_bias,
+    gather_in,
+    window_in,
+    scatter_in,
     h_out,
     spat_out,
     we_out,
     epi_out,
+    edge_out,
     img,
     listed,
     counts,
@@ -49,16 +100,29 @@
     ws,
     wa,
     wb,
+    wat,
+    wbt,
     we,
     gb,
     mk,
     rb,
     row_send,
     row_recv,
-    edge_send,
-    edge_recv,
+    gather,
+    window,
+    scatter,
+    col_send,
+    col_recv,
+    lines_send,
+    lines_recv,
+    diag_send,
+    diag_recv,
+    rows_ready,
+    cols_ready,
     img_sem,
     w_sem,
+    edge_send_sem,
+    edge_recv_sem,
     w_send_sem,
     w_recv_sem,
     send_sem,
@@ -87,9 +151,23 @@
     def greet(other):
         pl.semaphore_signal(barrier, inc=1, device_id=other, device_id_type=MESH)
 
-    greet(peer)
+    pl.when(seg == 0)(functools.partial(greet, peer))
     for i, j, there in around:
-        pl.when(there)(functools.partial(greet, at(i, j)))
+        core = 1 if j == 0 else 0
+        pl.when(there)(functools.partial(greet, {"segment": core, **at(i, j)}))
+
+    def meet(core, count, ready):
+        @pl.when(seg == core)
+        def _():
+            pl.semaphore_wait(barrier, count)
+            pl.semaphore_signal(ready, inc=1, device_id=peer, device_id_type=MESH)
+
+        @pl.when(seg != core)
+        def _():
+            pl.semaphore_wait(ready, 1)
+
+    def number(pick):
+        return sum((there.astype(jnp.int32) for _, j, there in around if pick(j)), 0)
 
     def image_load(s):
         return pltpu.make_async_copy(images.at[seg * slides + s], img.at[s], img_sem.at[s])
@@ -107,16 +185,19 @@
                 (outer_bias, ob),
                 (tissue_count, counts),
                 (tissue_list, listed),
+                (gather_in, gather),
+                (window_in, window),
+                (scatter_in, scatter),
             )
         )
     ]
-    for load in own[3:] + own[:1]:
+    for load in own[3:9] + own[:1]:
         load.start()
     for s in range(slides):
         image_load(s).start()
-    for load in own[1:3]:
+    for load in own[1:3] + own[9:]:
         load.start()
-    for load in own[3:]:
+    for load in own[3:9]:
         load.wait()
 
     lines = [ig[0].astype(F32), ib[0].astype(F32)]
@@ -129,16 +210,13 @@
     for s in range(slides):
         slide = seg * slides + s
         here = listed[pl.ds(slide, 1), :]
-        for t in range(cols // TW):
-            tile = col * (cols // TW) + t
+        for t in range(cols // TW + 2):
+            tile = col * (cols // TW) + t - 1
             hit = (here == tile) & (position < counts[slide])
             one = jnp.max(jnp.where(hit, 1.0, 0.0), axis=1, keepdims=True)
             mk[s, t] = jnp.broadcast_to(one, mk.shape[2:])
 
-    partners = 1
-    for _, _, there in around:
-        partners = partners + there.astype(jnp.int32)
-    pl.semaphore_wait(barrier, partners)
+    meet(1, 1 + 2 * number(lambda j: j == 0), rows_ready)
 
     def swap(src, dst, i):
         return remote(
@@ -160,20 +238,35 @@
         copy.start()
 
     def sends(e, s):
+        for n, (i, j, there) in enumerate(around[:2]):
+            yield there, remote(
+                src_ref=row_send.at[e, s, n],
+                dst_ref=row_recv.at[e, s, 1 - n],
+                send_sem=send_sem.at[e, s, n],
+                recv_sem=recv_sem.at[e, s, 1 - n],
+                device_id=at(i, j),
+                device_id_type=MESH,
+            )
+
+    def edge_sends():
         for n, (i, j, there) in enumerate(around):
+            a, b = (1 + i) // 2, (1 + j) // 2
             if j == 0:
-                src, dst = row_send.at[e, s, n], row_recv.at[e, s, 1 - n]
+                src, dst, here = lines_send.at[a], lines_recv.at[1 - a], lines_recv.at[a]
+            elif i == 0:
+                src, dst, here = col_send.at[b], col_recv.at[1 - b], col_recv.at[b]
             else:
-                src = edge_send.at[e, s, (1 + j) // 2]
-                dst = edge_recv.at[e, s, (1 - j) // 2 * 3 + (i + 2 if i == 0 else (1 - i) // 2)]
-            yield there, remote(
+                src, dst = diag_send.at[a, b], diag_recv.at[1 - a, 1 - b]
+                here = diag_recv.at[a, b]
+            copy = remote(
                 src_ref=src,
                 dst_ref=dst,
-                send_sem=send_sem.at[e, s, n],
-                recv_sem=recv_sem.at[e, s, mirror(n)],
+                send_sem=edge_send_sem.at[n],
+                recv_sem=edge_recv_sem.at[mirror(n)],
                 device_id=at(i, j),
                 device_id_type=MESH,
             )
+            yield there, copy, here
 
     def mirror(n):
         i, j, _ = around[n]
@@ -194,7 +287,7 @@
         v = jnp.dot(
             x.reshape(pairs * cols, chans), wr[e], preferred_element_type=F32
         ).reshape(pairs, cols // TW, TW, inner)
-        mask = mk[s][:, 0:1]
+        mask = mk[s, 1 : 1 + cols // TW][:, 0:1]
         gain = (gb[e, 0:1] * mask)[None]
         bias = (gb[e, 2:3] * mask)[None]
         red = jnp.maximum(v * gain + bias, 0.0).reshape(pairs, cols, inner)
@@ -202,8 +295,6 @@
             row_send[e, s, 0] = red[0].astype(BF16)
         else:
             row_send[e, s, 1] = red[pairs - 1].astype(BF16)
-        edge_send[e, s, 0, pl.ds(half * pairs, pairs)] = red[:, 0]
-        edge_send[e, s, 1, pl.ds(half * pairs, pairs)] = red[:, last]
         return red
 
     def send(e, s):
@@ -213,38 +304,17 @@
     def halo(e, s):
         copies = list(sends(e, s))
         for n, (there, _) in enumerate(copies):
-            pl.when(there)(copies[mirror(n)][1].wait_recv)
-        above, below = row > 0, row < n_row - 1
-        at_left, at_right = col > 0, col < n_col - 1
-        place = lax.broadcasted_iota(jnp.int32, (cols, inner), 0)
-        spot = lax.broadcasted_iota(jnp.int32, (16, inner), 0)
-        zero = jnp.zeros((1, inner), F32)
-
-        def beyond(side, slot, line, there):
-            pixel = edge_recv[e, s, 3 * side + slot, line : line + 1]
-            return jnp.where(there & (at_right if side else at_left), pixel, zero)
-
-        for way, there, slot, line, q, lane in (
-            (0, above, 0, 2 * pairs - 1, 0, 0),
-            (1, below, 1, 0, pairs, 3 * inner),
-        ):
+            pl.when(there)(copies[1 - n][1].wait_recv)
+        for way, there, q, lane in ((0, row > 0, 0, 0), (1, row < n_row - 1, pairs, 3 * inner)):
             got = jnp.where(there, row_recv[e, s, way].astype(F32), 0.0)
-            before = jnp.where(place == 0, beyond(0, slot, line, there), pltpu.roll(got, 1, 0))
-            after = jnp.where(place == last, beyond(1, slot, line, there), pltpu.roll(got, last, 0))
             rb[e, s, q, :, lane : lane + 3 * inner] = jnp.concatenate(
-                [before.astype(BF16), got.astype(BF16), after.astype(BF16)], axis=1
-            )
-        for half in range(2):
-            for p in range(pairs):
-                line, lane = half * pairs + p, (1 - half) * 3 * inner
-                here = rb.at[e, s, p + half, 0:16, lane : lane + inner]
-                here[...] = jnp.where(
-                    spot == 0, beyond(0, 2, line, True), here[...].astype(F32)
-                ).astype(BF16)
-                here = rb.at[e, s, p + half, cols - 16 : cols, lane + 2 * inner : lane + 3 * inner]
-                here[...] = jnp.where(
-                    spot == 15, beyond(1, 2, line, True), here[...].astype(F32)
-                ).astype(BF16)
+                [
+                    pltpu.roll(got, 1, 0).astype(BF16),
+                    got.astype(BF16),
+                    pltpu.roll(got, last, 0).astype(BF16),
+                ],
+                axis=1,
+            )
 
     def spatial(e, s):
         total = jnp.dot(
@@ -260,13 +330,18 @@
     def spread(b):
         depth = 3 * inner
         zero = jnp.zeros((depth, inner), BF16)
-        w = [ws[b, dy].reshape(depth, inner) for dy in range(3)]
-        wa[b] = jnp.concatenate(
-            [jnp.concatenate([w[0], zero], axis=1), jnp.concatenate([w[1], w[0]], axis=1)], axis=0
-        )
-        wb[b] = jnp.concatenate(
-            [jnp.concatenate([w[2], w[1]], axis=1), jnp.concatenate([zero, w[2]], axis=1)], axis=0
-        )
+        for w, first, second in (
+            ([ws[b, i].reshape(depth, inner) for i in range(3)], wa, wb),
+            ([ws[b, :, i].reshape(depth, inner) for i in range(3)], wat, wbt),
+        ):
+            first[b] = jnp.concatenate(
+                [jnp.concatenate([w[0], zero], axis=1), jnp.concatenate([w[1], w[0]], axis=1)],
+                axis=0,
+            )
+            second[b] = jnp.concatenate(
+                [jnp.concatenate([w[2], w[1]], axis=1), jnp.concatenate([zero, w[2]], axis=1)],
+                axis=0,
+            )
 
     def outer(b):
         n = chans // inner
@@ -274,12 +349,160 @@
         bias = jnp.concatenate([gb[b, 4 + n + i : 5 + n + i] for i in range(n)], axis=1)
         return gain, bias
 
+    def edge_pixels(s, side):
+        cells = img[s, :, :, side * (cols - 16) : side * (cols - 16) + 16]
+        return cells.reshape(2 * pairs * 16, chans)
+
+    def send_edges():
+        meet(0, 2 * number(lambda j: j != 0), cols_ready)
+        parts = []
+        for s in range(slides):
+            parts.append(
+                [
+                    jnp.dot(gather[side], edge_pixels(s, side), preferred_element_type=F32)
+                    for side in range(2)
+                ]
+            )
+            for side in range(2):
+                col_send[side, s] = parts[s][side][0:16].astype(BF16)
+            for way in range(2):
+                cut = slice(16 + 8 * way, 24 + 8 * way)
+                lines_send[way, s] = jnp.concatenate(
+                    [parts[s][0][cut], parts[s][1][cut]], axis=0
+                ).astype(BF16)
+        for way in range(2):
+            cut = slice(32 + 8 * way, 40 + 8 * way)
+            for side in range(2):
+                for t in range(2):
+                    two = [parts[min(2 * t + i, slides - 1)][side][cut] for i in range(2)]
+                    diag_send[way, side, t] = jnp.concatenate(two, axis=0).astype(BF16)
+        for there, copy, _ in edge_sends():
+            pl.when(there)(copy.start)
+
+    def edge_strips():
+        copies = list(edge_sends())
+        for n, (there, _, here) in enumerate(copies):
+            pl.when(there)(copies[mirror(n)][1].wait_recv)
+
+            @pl.when(jnp.logical_not(there))
+            def _():
+                here[...] = jnp.zeros_like(here)
+
+        strips = 2 * slides
+        own_row = lax.broadcasted_iota(jnp.int32, (16, inner), 0)
+        valid = jnp.where(
+            own_row < 8,
+            1.0,
+            jnp.where(
+                own_row < 14,
+                jnp.where(row < n_row - 1, 1.0, 0.0),
+                jnp.where(row > 0, 1.0, 0.0),
+            ),
+        )
+        cells, masks = [], []
+        for s in range(slides):
+            for side in range(2):
+                mine = edge_pixels(s, side)
+                source = jnp.concatenate(
+                    [
+                        mine,
+                        col_recv[side, s],
+                        lines_recv[0, s],
+                        lines_recv[1, s],
+                        diag_recv[0, side, s // 2],
+                        diag_recv[1, side, s // 2],
+                        mine[0:48],
+                    ],
+                    axis=0,
+                )
+                got = jnp.dot(window[2 * side + s % 2], source, preferred_element_type=F32)
+                cells.append(got.astype(BF16).reshape(1, 6, 16, chans))
+                tiles = (2, 2, 2, 2, 3, 3) if side else (0, 0, 1, 1, 1, 1)
+                masks.append([mk[s, t, 0:1] for t in tiles])
+        x = jnp.concatenate(cells, axis=0)
+
+        def mask_of(columns):
+            return jnp.concatenate(
+                [jnp.stack([m[w] * valid for w in columns])[None] for m in masks], axis=0
+            )
+
+        def reduced(e, x, columns):
+            n = len(columns)
+            v = jnp.dot(x.reshape(-1, chans), wr[e], preferred_element_type=F32)
+            v = jnp.maximum(v * gb[e, 0:1] + gb[e, 2:3], 0.0)
+            v = v.reshape(strips, n, 16, inner) * mask_of(columns)
+            flat = v.reshape(strips * n, 16, inner)
+            return jnp.concatenate(
+                [
+                    pltpu.roll(flat, 1, 1).astype(BF16),
+                    flat.astype(BF16),
+                    pltpu.roll(flat, 15, 1).astype(BF16),
+                ],
+                axis=2,
+            ).reshape(strips, n, 16, 3 * inner)
+
+        def conv(e, first, second):
+            total = jnp.dot(first, wat[e], preferred_element_type=F32)
+            total += jnp.dot(second, wbt[e], preferred_element_type=F32)
+            gain, bias = widen(gb[e, 1:2], 2), widen(gb[e, 3:4], 2)
+            return jnp.maximum(total * gain + bias, 0.0)
+
+        def expanded(e, sp, h, mask):
+            gain, bias = outer(e)
+            z = jnp.dot(sp, we[e], preferred_element_type=F32).reshape(h.shape)
+            z = jnp.maximum(z * gain + bias + h.astype(F32), 0.0)
+            return z * mask
+
+        r = reduced(0, x, range(6))
+        two = [jnp.concatenate([r[:, 2 * i], r[:, 2 * i + 1]], axis=2)[:, None] for i in range(3)]
+        sp = conv(
+            0,
+            jnp.concatenate(two[0:2], axis=1).reshape(-1, 6 * inner),
+            jnp.concatenate(two[1:3], axis=1).reshape(-1, 6 * inner),
+        ).astype(BF16)
+        h, red = [], []
+        for half in range(2):
+            columns = (1 + half, 3 + half)
+            before = jnp.concatenate([x[:, w][:, None] for w in columns], axis=1)
+            mask = jnp.concatenate(
+                [
+                    jnp.stack([jnp.broadcast_to(widen(m[w], chans // inner), (16, chans)) for w in columns])[None]
+                    for m in masks
+                ],
+                axis=0,
+            )
+            now = expanded(0, sp[:, half * inner : (half + 1) * inner], before, mask)
+            h.append(now)
+            red.append(reduced(1, now.astype(BF16), columns))
+        first, second = (
+            jnp.concatenate([red[0][:, i], red[1][:, i]], axis=2).reshape(-1, 6 * inner)
+            for i in range(2)
+        )
+        sp = conv(1, first, second).reshape(strips, 16, 2 * inner)[:, 0:8]
+        done = []
+        for half in range(2):
+            now = h[1 - half][:, half, 0:8].astype(BF16)
+            mask = jnp.concatenate([widen(m[2 + half], chans // inner)[None] for m in masks], axis=0)
+            z = sp[:, :, half * inner : (half + 1) * inner].reshape(strips * 8, inner)
+            done.append(expanded(1, z.astype(BF16), now, mask)[:, None])
+        done = jnp.concatenate(done, axis=1).reshape(strips * 16, chans).astype(BF16)
+        done = jnp.concatenate([done, jnp.zeros((128 - strips * 16, chans), BF16)], axis=0)
+        for i in range(strips):
+            put = jnp.dot(scatter[i], done, preferred_element_type=F32).astype(BF16)
+            edge_out[i] = put.reshape(pairs, 2, 16, chans)
+
+    late = lax.rem(col, RUN) == 0
+    for load in own[9:]:
+        load.wait()
+    for s in range(slides):
+        image_load(s).wait()
+    pl.when(jnp.logical_not(late))(send_edges)
+
     own[0].wait()
     for copy in swaps[:2]:
         copy.wait()
 
     def first_reduce(s, carry):
-        image_load(s).wait()
         reds = [reduce_half(0, s, half, img[s, :, half]) for half in range(2)]
         send(0, s)
         for half in range(2):
@@ -299,7 +522,7 @@
         halo(0, s)
         sp = spatial(0, s)
         gain, bias = outer(0)
-        mask = widen(mk[s][:, 0:1].reshape(cols // TW, inner), chans // inner)[:, None]
+        mask = widen(mk[s, 1 : 1 + cols // TW][:, 0:1].reshape(cols // TW, inner), chans // inner)[:, None]
         reds = []
         for half in range(2):
             z = jnp.dot(
@@ -326,10 +549,15 @@
     gain, bias = outer(1)
     for s in range(slides):
         for t in range(cols // TW):
-            mask = widen(mk[s, t, 0:1], chans // inner)
+            mask = widen(mk[s, t + 1, 0:1], chans // inner)
             epi_out[s, t : t + 1] = gain * mask
             epi_out[s, 2 + t : 3 + t] = bias * mask
     lax.fori_loop(0, slides, final, 0)
+
+    pl.when(late)(send_edges)
+    edge_strips()
+    for there, copy, _ in edge_sends():
+        pl.when(there)(copy.wait_send)
 
     def drain(s, carry):
         for e in range(2):
@@ -340,7 +568,7 @@
     lax.fori_loop(0, slides, drain, 0)
 
 
-def expand_kernel(h, spat, we, epi, out, held, sem):
+def expand_kernel(h, spat, we, epi, edge, out, held, sem):
     slides, pairs, _, cols, chans = h.shape
     inner = we.shape[0]
     tiles = cols // TW
@@ -356,6 +584,11 @@
             bias = epi[s, 2 : 2 + tiles][None, :, None]
             z = z * gain + bias + h[s, :, half].astype(F32).reshape(pairs, tiles, TW, chans)
             held[s, :, half] = jnp.maximum(z, 0.0).astype(BF16).reshape(pairs, cols, chans)
+        place = lax.broadcasted_iota(jnp.int32, (pairs, 2, 16, chans), 2)
+        for side in range(2):
+            here = held.at[s, :, :, side * (cols - 16) : side * (cols - 16) + 16]
+            edges = place >= 14 if side else place < 2
+            here[...] = jnp.where(edges, edge[2 * s + side].astype(F32), here[...].astype(F32)).astype(BF16)
         pltpu.make_async_copy(held.at[s], out.at[s], sem.at[s]).start()
         return carry
 
@@ -370,19 +603,21 @@
     inner = weights[0].shape[2]
     w_reduce, w_spatial, w_expand, inner_gain, inner_bias, outer_gain, outer_bias = weights
     w_spatial = w_spatial.reshape(1, 3, 3, inner, inner)
+    picks = [jnp.asarray(x) for x in selections(rows)]
     hbm = pl.BlockSpec(memory_space=pltpu.HBM)
     vmem = pl.BlockSpec(memory_space=pltpu.VMEM)
     dma = pltpu.SemaphoreType.DMA
-    h, spat, we, epi = pl.pallas_call(
+    h, spat, we, epi, edge = pl.pallas_call(
         functools.partial(blocks_kernel, grid),
         out_shape=(
             pltpu.VMEM((slides, pairs, 2, cols, chans), BF16),
             pltpu.VMEM((slides, pairs, cols, 2 * inner), BF16),
             pltpu.VMEM((inner, chans), BF16),
             pltpu.VMEM((slides, 4, chans), F32),
+            pltpu.VMEM((2 * slides, pairs, 2, 16, chans), BF16),
         ),
-        in_specs=[hbm] * 10,
-        out_specs=(vmem,) * 4,
+        in_specs=[hbm] * 13,
+        out_specs=(vmem,) * 5,
         scratch_shapes=[
             pltpu.VMEM((slides, pairs, 2, cols, chans), BF16),
             pltpu.VMEM(tissue_list.shape, jnp.int32),
@@ -393,22 +628,26 @@
             pltpu.VMEM(outer_bias.shape, BF16),
             pltpu.VMEM((2, chans, inner), BF16),
             pltpu.VMEM((2, 3, 3, inner, inner), BF16),
-            pltpu.VMEM((2, 6 * inner, 2 * inner), BF16),
-            pltpu.VMEM((2, 6 * inner, 2 * inner), BF16),
+            *[pltpu.VMEM((2, 6 * inner, 2 * inner), BF16)] * 4,
             pltpu.VMEM((2, inner, chans), BF16),
             pltpu.VMEM((2, 16, inner), F32),
-            pltpu.VMEM((slides, cols // TW, 8, inner), F32),
+            pltpu.VMEM((slides, cols // TW + 2, 8, inner), F32),
             pltpu.VMEM((2, slides, pairs + 1, cols, 6 * inner), BF16),
             pltpu.VMEM((2, slides, 2, cols, inner), BF16),
             pltpu.VMEM((2, slides, 2, cols, inner), BF16),
-            pltpu.VMEM((2, slides, 2, rows, inner), F32),
-            pltpu.VMEM((2, slides, 6, rows, inner), F32),
+            *[pltpu.VMEM(x.shape, BF16) for x in picks],
+            *[pltpu.VMEM((2, slides, 16, chans), BF16)] * 4,
+            *[pltpu.VMEM((2, 2, 2, 16, chans), BF16)] * 2,
+            pltpu.SemaphoreType.REGULAR,
+            pltpu.SemaphoreType.REGULAR,
             dma((slides,)),
-            dma((9,)),
+            dma((12,)),
+            dma((8,)),
+            dma((8,)),
             dma((4,)),
             dma((4,)),
-            dma((2, slides, 8)),
-            dma((2, slides, 8)),
+            dma((2, slides, 2)),
+            dma((2, slides, 2)),
         ],
         compiler_params=pltpu.CompilerParams(
             collective_id=0, has_side_effects=True, vmem_limit_bytes=40 * 2**20
@@ -428,13 +667,14 @@
                 inner_bias,
                 outer_gain,
                 outer_bias,
+                *picks,
             )
         )
     )
     out = pl.pallas_call(
         expand_kernel,
         out_shape=jax.ShapeDtypeStruct((slides, pairs, 2, cols, chans), BF16),
-        in_specs=[vmem] * 4,
+        in_specs=[vmem] * 5,
         out_specs=hbm,
         scratch_shapes=[
             pltpu.VMEM((slides, pairs, 2, cols, chans), BF16),
@@ -442,7 +682,7 @@
         ],
         compiler_params=pltpu.CompilerParams(vmem_limit_bytes=24 * 2**20),
         name="expand",
-    )(h, spat, we, epi)
+    )(h, spat, we, epi, edge)
     return out.reshape(slides, rows, cols, chans)
 
 

time: 27.9 us -> 28.1 us (level)
  the two profiles are of different devices: /device:TPU:24 before, /device:TPU:1 now
where the time goes in v3:
time: 28.1 us; the launch traced here: 28 us
  Pallas kernels  28 us (100%)
    pallas_call x1, Pallas kernels, shards(): pl.pallas_call(functools.partial(blocks_kernel, grid), out_shape=(pltpu.V...  25.4 us
    pallas_call x1, Pallas kernels, shards(): pl.pallas_call(expand_kernel, out_shape=jax.ShapeDtypeStruct((slides, pai...  2.61 us

profile of v3, /device:TPU:1, one launch (start us, length us, event | category | flops | bytes accessed | tf_op | source)
XLA Modules:
  0.0 28.0 jit_solution(16105619058338621511)
XLA Ops:
  0.0 25.4 %blocks.1 = (bf16[3,4,2,128,512]{4,3,2,1,0:T(8,128)(2,1)S(1)}, bf16[3,4,128,256]{3,2,1,0:T(8,128)(2,1)S(1)}, bf16[128,512]{1,0:T(8,128)(2,1)S(1)}, f32[3,4,512]{...) custom-call(bf16[6,4,2,128,512]{4,3,2,1,0:T(8,128)(2,1)} %bitcast.2, s32[6,64]{1,0:T(8,128)} %tissue_list.1, s32[6]{0:T(128)} %tissue_count.1, ...), custom_call_target="tpu_custom_call" | custom-call | tf_op jit(solution)/shard_map/blocks/pallas_call | solution.py:610
  25.4 2.6 %expand.1 = bf16[3,4,2,128,512]{4,3,2,1,0:T(8,128)(2,1)} custom-call(bf16[3,4,2,128,512]{4,3,2,1,0:T(8,128)(2,1)S(1)} %get-tuple-element.10.h, bf16[3,4,128,256]{3,2,1,0:T(8,128)(2,1)S(1)} %get-tuple-element.11.spat, bf16[128,512]{1,0:T(8,128)(2,1)S(1)} %get-tuple-element.12.we, f32[3,4,512]{2,1,0:T(4,128)S(1)} %get-tuple-element.13.epi, ...), custom_call_target="tpu_custom_call" | custom-call | tf_op jit(solution)/shard_map/expand/pallas_call | solution.py:674

commit v4 on v3

--- a/solution.py
+++ b/solution.py
@@ -57,7 +57,8 @@
             for q in range(2):
                 for r in range(rows):
                     scatter[strip, r * 16 + 14 * side + q, strip * 16 + q * 8 + r] = 1
-    window = window.reshape(4, 96, 256)
+    window = window.reshape(4, 96, 2, 128).swapaxes(1, 2)
+    window = window.reshape(8, 96, 128)
     return [x.astype(ml_dtypes.bfloat16) for x in (gather, window, scatter)]
 
 
@@ -84,12 +85,9 @@
     gather_in,
     window_in,
     scatter_in,
-    h_out,
-    spat_out,
-    we_out,
-    epi_out,
-    edge_out,
+    out,
     img,
+    mid,
     listed,
     counts,
     ig,
@@ -237,13 +235,13 @@
     for copy in swaps:
         copy.start()
 
-    def sends(e, s):
+    def row_sends(e):
         for n, (i, j, there) in enumerate(around[:2]):
             yield there, remote(
-                src_ref=row_send.at[e, s, n],
-                dst_ref=row_recv.at[e, s, 1 - n],
-                send_sem=send_sem.at[e, s, n],
-                recv_sem=recv_sem.at[e, s, 1 - n],
+                src_ref=row_send.at[e, n],
+                dst_ref=row_recv.at[e, 1 - n],
+                send_sem=send_sem.at[e, n],
+                recv_sem=recv_sem.at[e, 1 - n],
                 device_id=at(i, j),
                 device_id_type=MESH,
             )
@@ -272,9 +270,9 @@
         i, j, _ = around[n]
         return [(a, b) for a, b, _ in around].index((-i, -j))
 
-    def store_shifted(e, s, half, red):
-        place = rb.at[e, s, pl.ds(half, pairs), :, pl.ds((1 - half) * 3 * inner, 3 * inner)]
-        place[...] = jnp.concatenate(
+    def place_row(e, r, red):
+        lane = (r + 1) % 2 * 3 * inner
+        rb[e, :, (r + 1) // 2, :, lane : lane + 3 * inner] = jnp.concatenate(
             [
                 pltpu.roll(red, 1, 1).astype(BF16),
                 red.astype(BF16),
@@ -283,49 +281,42 @@
             axis=2,
         )
 
-    def reduce_half(e, s, half, x):
-        v = jnp.dot(
-            x.reshape(pairs * cols, chans), wr[e], preferred_element_type=F32
-        ).reshape(pairs, cols // TW, TW, inner)
-        mask = mk[s, 1 : 1 + cols // TW][:, 0:1]
-        gain = (gb[e, 0:1] * mask)[None]
-        bias = (gb[e, 2:3] * mask)[None]
-        red = jnp.maximum(v * gain + bias, 0.0).reshape(pairs, cols, inner)
-        if half == 0:
-            row_send[e, s, 0] = red[0].astype(BF16)
-        else:
-            row_send[e, s, 1] = red[pairs - 1].astype(BF16)
-        return red
-
-    def send(e, s):
-        for there, copy in sends(e, s):
-            pl.when(there)(copy.start)
-
-    def halo(e, s):
-        copies = list(sends(e, s))
+    def reduce_pair(e, x, p):
+        v = jnp.dot(x.reshape(-1, chans), wr[e], preferred_element_type=F32)
+        v = v.reshape(slides, 2, cols // TW, TW, inner)
+        mask = mk[:, 1 : 1 + cols // TW, 0:1][:, None]
+        red = jnp.maximum(v * (gb[e, 0:1] * mask) + gb[e, 2:3] * mask, 0.0)
+        return red.reshape(slides, 2, cols, inner)
+
+    def send_row(e, way, red):
+        row_send[e, way] = red[:, way].astype(BF16)
+        there, copy = list(row_sends(e))[way]
+        pl.when(there)(copy.start)
+
+    def halo(e):
+        copies = list(row_sends(e))
         for n, (there, _) in enumerate(copies):
             pl.when(there)(copies[1 - n][1].wait_recv)
-        for way, there, q, lane in ((0, row > 0, 0, 0), (1, row < n_row - 1, pairs, 3 * inner)):
-            got = jnp.where(there, row_recv[e, s, way].astype(F32), 0.0)
-            rb[e, s, q, :, lane : lane + 3 * inner] = jnp.concatenate(
-                [
-                    pltpu.roll(got, 1, 0).astype(BF16),
-                    got.astype(BF16),
-                    pltpu.roll(got, last, 0).astype(BF16),
-                ],
-                axis=1,
-            )
-
-    def spatial(e, s):
-        total = jnp.dot(
-            rb[e, s, 0:pairs].reshape(pairs * cols, 6 * inner), wa[e], preferred_element_type=F32
-        ) + jnp.dot(
-            rb[e, s, 1 : pairs + 1].reshape(pairs * cols, 6 * inner),
-            wb[e],
-            preferred_element_type=F32,
-        )
+        for way, there, r in ((0, row > 0, -1), (1, row < n_row - 1, 2 * pairs)):
+            place_row(e, r, jnp.where(there, row_recv[e, way].astype(F32), 0.0))
+
+    def spatial(e, p):
+        total = jnp.dot(rb[e, :, p].reshape(-1, 6 * inner), wa[e], preferred_element_type=F32)
+        total += jnp.dot(rb[e, :, p + 1].reshape(-1, 6 * inner), wb[e], preferred_element_type=F32)
         gain, bias = widen(gb[e, 1:2], 2), widen(gb[e, 3:4], 2)
         return jnp.maximum(total * gain + bias, 0.0).astype(BF16)
+
+    def expand(e, sp, p, before, after):
+        gain, bias = outer(e)
+        mask = mk[:, 1 : 1 + cols // TW, 0:1]
+        mask = jnp.concatenate([mask] * (chans // inner), axis=3)
+        for half in range(2):
+            z = jnp.dot(
+                sp[:, half * inner : (half + 1) * inner], we[e], preferred_element_type=F32
+            ).reshape(slides, cols, chans)
+            y = jnp.maximum(z * gain + bias + before[:, p, half].astype(F32), 0.0)
+            y = y.reshape(slides, cols // TW, TW, chans) * mask
+            after[:, p, half] = y.reshape(slides, cols, chans).astype(BF16)
 
     def spread(b):
         depth = 3 * inner
@@ -415,7 +406,9 @@
                     ],
                     axis=0,
                 )
-                got = jnp.dot(window[2 * side + s % 2], source, preferred_element_type=F32)
+                k = 4 * side + 2 * (s % 2)
+                pick = jnp.concatenate([window[k], window[k + 1]], axis=1)
+                got = jnp.dot(pick, source, preferred_element_type=F32)
                 cells.append(got.astype(BF16).reshape(1, 6, 16, chans))
                 tiles = (2, 2, 2, 2, 3, 3) if side else (0, 0, 1, 1, 1, 1)
                 masks.append([mk[s, t, 0:1] for t in tiles])
@@ -488,8 +481,11 @@
         done = jnp.concatenate(done, axis=1).reshape(strips * 16, chans).astype(BF16)
         done = jnp.concatenate([done, jnp.zeros((128 - strips * 16, chans), BF16)], axis=0)
         for i in range(strips):
-            put = jnp.dot(scatter[i], done, preferred_element_type=F32).astype(BF16)
-            edge_out[i] = put.reshape(pairs, 2, 16, chans)
+            put = jnp.dot(scatter[i], done, preferred_element_type=F32).reshape(pairs, 2, 16, chans)
+            spot = lax.broadcasted_iota(jnp.int32, put.shape, 2)
+            here = out.at[i // 2, :, :, i % 2 * (cols - 16) : i % 2 * (cols - 16) + 16]
+            edges = spot >= 14 if i % 2 else spot < 2
+            here[...] = jnp.where(edges, put, here[...].astype(F32)).astype(BF16)
 
     late = lax.rem(col, RUN) == 0
     for load in own[9:]:
@@ -501,15 +497,25 @@
     own[0].wait()
     for copy in swaps[:2]:
         copy.wait()
-
-    def first_reduce(s, carry):
-        reds = [reduce_half(0, s, half, img[s, :, half]) for half in range(2)]
-        send(0, s)
-        for half in range(2):
-            store_shifted(0, s, half, reds[half])
-        return carry
-
-    lax.fori_loop(0, slides, first_reduce, 0)
+    ends = (0, pairs - 1)
+    between = tuple(range(1, pairs - 1))
+
+    def place_pairs(e, group, reds):
+        for p, red in zip(group, reds):
+            for half in range(2):
+                place_row(e, 2 * p + half, red[:, half])
+
+    def reduce_ends(e, x):
+        reds = [reduce_pair(e, x[:, p], p) for p in ends]
+        for way in range(2):
+            send_row(e, way, reds[way])
+        place_pairs(e, ends, reds)
+
+    def reduce_between(e, x):
+        place_pairs(e, between, [reduce_pair(e, x[:, p], p) for p in between])
+
+    reduce_ends(0, img)
+    reduce_between(0, img)
 
     for load in own[1:3]:
         load.wait()
@@ -518,83 +524,36 @@
     spread(0)
     spread(1)
 
-    def middle(s, carry):
-        halo(0, s)
-        sp = spatial(0, s)
-        gain, bias = outer(0)
-        mask = widen(mk[s, 1 : 1 + cols // TW][:, 0:1].reshape(cols // TW, inner), chans // inner)[:, None]
-        reds = []
-        for half in range(2):
-            z = jnp.dot(
-                sp[:, half * inner : (half + 1) * inner], we[0], preferred_element_type=F32
-            ).reshape(pairs, cols, chans)
-            z = z * gain + bias + img[s, :, half].astype(F32)
-            z = jnp.maximum(z, 0.0).reshape(pairs, cols // TW, TW, chans) * mask[None]
-            z = z.astype(BF16).reshape(pairs, cols, chans)
-            h_out[s, :, half] = z
-            reds.append(reduce_half(1, s, half, z))
-        send(1, s)
-        for half in range(2):
-            store_shifted(1, s, half, reds[half])
-        return carry
-
-    lax.fori_loop(0, slides, middle, 0)
-
-    def final(s, carry):
-        halo(1, s)
-        spat_out[s] = spatial(1, s).reshape(pairs, cols, 2 * inner)
-        return carry
-
-    we_out[...] = we[1]
-    gain, bias = outer(1)
-    for s in range(slides):
-        for t in range(cols // TW):
-            mask = widen(mk[s, t + 1, 0:1], chans // inner)
-            epi_out[s, t : t + 1] = gain * mask
-            epi_out[s, 2 + t : 3 + t] = bias * mask
-    lax.fori_loop(0, slides, final, 0)
+    def expand_pairs(e, group, before, after):
+        parts = [spatial(e, p) for p in group]
+        for p, sp in zip(group, parts):
+            expand(e, sp, p, before, after)
+
+    expand_pairs(0, between, img, mid)
+    reduce_between(1, mid)
+    halo(0)
+    expand_pairs(0, ends, img, mid)
+    reduce_ends(1, mid)
+    expand_pairs(1, between, mid, out)
+    halo(1)
+    expand_pairs(1, ends, mid, out)
 
     pl.when(late)(send_edges)
     edge_strips()
     for there, copy, _ in edge_sends():
         pl.when(there)(copy.wait_send)
 
-    def drain(s, carry):
-        for e in range(2):
-            for there, copy in sends(e, s):
-                pl.when(there)(copy.wait_send)
-        return carry
-
-    lax.fori_loop(0, slides, drain, 0)
-
-
-def expand_kernel(h, spat, we, epi, edge, out, held, sem):
-    slides, pairs, _, cols, chans = h.shape
-    inner = we.shape[0]
-    tiles = cols // TW
-
-    def one(s, carry):
-        for half in range(2):
-            z = jnp.dot(
-                spat[s].reshape(pairs * cols, 2 * inner)[:, half * inner : (half + 1) * inner],
-                we[...],
-                preferred_element_type=F32,
-            ).reshape(pairs, tiles, TW, chans)
-            gain = epi[s, 0:tiles][None, :, None]
-            bias = epi[s, 2 : 2 + tiles][None, :, None]
-            z = z * gain + bias + h[s, :, half].astype(F32).reshape(pairs, tiles, TW, chans)
-            held[s, :, half] = jnp.maximum(z, 0.0).astype(BF16).reshape(pairs, cols, chans)
-        place = lax.broadcasted_iota(jnp.int32, (pairs, 2, 16, chans), 2)
-        for side in range(2):
-            here = held.at[s, :, :, side * (cols - 16) : side * (cols - 16) + 16]
-            edges = place >= 14 if side else place < 2
-            here[...] = jnp.where(edges, edge[2 * s + side].astype(F32), here[...].astype(F32)).astype(BF16)
-        pltpu.make_async_copy(held.at[s], out.at[s], sem.at[s]).start()
-        return carry
-
-    lax.fori_loop(0, slides, one, 0)
-    for s in range(slides):
-        pltpu.make_async_copy(held.at[s], out.at[s], sem.at[s]).wait()
+    for e in range(2):
+        for there, copy in row_sends(e):
+            pl.when(there)(copy.wait_send)
+
+
+def write_kernel(held, out, sem):
+    copies = [pltpu.make_async_copy(held.at[s], out.at[s], sem.at[s]) for s in range(held.shape[0])]
+    for copy in copies:
+        copy.start()
+    for copy in copies:
+        copy.wait()
 
 
 def shards(grid, images, tissue_list, tissue_count, *weights):
@@ -607,19 +566,13 @@
     hbm = pl.BlockSpec(memory_space=pltpu.HBM)
     vmem = pl.BlockSpec(memory_space=pltpu.VMEM)
     dma = pltpu.SemaphoreType.DMA
-    h, spat, we, epi, edge = pl.pallas_call(
+    held = pl.pallas_call(
         functools.partial(blocks_kernel, grid),
-        out_shape=(
-            pltpu.VMEM((slides, pairs, 2, cols, chans), BF16),
-            pltpu.VMEM((slides, pairs, cols, 2 * inner), BF16),
-            pltpu.VMEM((inner, chans), BF16),
-            pltpu.VMEM((slides, 4, chans), F32),
-            pltpu.VMEM((2 * slides, pairs, 2, 16, chans), BF16),
-        ),
+        out_shape=pltpu.VMEM((slides, pairs, 2, cols, chans), BF16),
         in_specs=[hbm] * 13,
-        out_specs=(vmem,) * 5,
+        out_specs=vmem,
         scratch_shapes=[
-            pltpu.VMEM((slides, pairs, 2, cols, chans), BF16),
+            *[pltpu.VMEM((slides, pairs, 2, cols, chans), BF16)] * 2,
             pltpu.VMEM(tissue_list.shape, jnp.int32),
             pltpu.SMEM(tissue_count.shape, jnp.int32),
             pltpu.VMEM(inner_gain.shape, BF16),
@@ -633,8 +586,7 @@
             pltpu.VMEM((2, 16, inner), F32),
             pltpu.VMEM((slides, cols // TW + 2, 8, inner), F32),
             pltpu.VMEM((2, slides, pairs + 1, cols, 6 * inner), BF16),
-            pltpu.VMEM((2, slides, 2, cols, inner), BF16),
-            pltpu.VMEM((2, slides, 2, cols, inner), BF16),
+            *[pltpu.VMEM((2, 2, slides, cols, inner), BF16)] * 2,
             *[pltpu.VMEM(x.shape, BF16) for x in picks],
             *[pltpu.VMEM((2, slides, 16, chans), BF16)] * 4,
             *[pltpu.VMEM((2, 2, 2, 16, chans), BF16)] * 2,
@@ -646,8 +598,8 @@
             dma((8,)),
             dma((4,)),
             dma((4,)),
-            dma((2, slides, 2)),
-            dma((2, slides, 2)),
+            dma((2, 2)),
+            dma((2, 2)),
         ],
         compiler_params=pltpu.CompilerParams(
             collective_id=0, has_side_effects=True, vmem_limit_bytes=40 * 2**20
@@ -672,17 +624,14 @@
         )
     )
     out = pl.pallas_call(
-        expand_kernel,
+        write_kernel,
         out_shape=jax.ShapeDtypeStruct((slides, pairs, 2, cols, chans), BF16),
-        in_specs=[vmem] * 5,
+        in_specs=[vmem],
         out_specs=hbm,
-        scratch_shapes=[
-            pltpu.VMEM((slides, pairs, 2, cols, chans), BF16),
-            dma((slides,)),
-        ],
-        compiler_params=pltpu.CompilerParams(vmem_limit_bytes=24 * 2**20),
-        name="expand",
-    )(h, spat, we, epi, edge)
+        scratch_shapes=[dma((slides,))],
+        compiler_params=pltpu.CompilerParams(vmem_limit_bytes=16 * 2**20),
+        name="write",
+    )(held)
     return out.reshape(slides, rows, cols, chans)
 
 

time: 28.1 us -> 26.2 us (0.932)
  Pallas kernels: 28 us -> 26.1 us
    pallas_call x2, Pallas kernels: 28 us -> 26.1 us  [the longest x1 24.4 us: shards(): pl.pallas_call(functools.partial(blocks_kernel, grid), out_shape=pltpu.VM...]
where the time goes in v4:
time: 26.2 us; the launch traced here: 26.1 us
  Pallas kernels  26.1 us (100%)
    pallas_call x1, Pallas kernels, shards(): pl.pallas_call(functools.partial(blocks_kernel, grid), out_shape=pltpu.VM...  24.4 us
    pallas_call x1, Pallas kernels, shards(): pl.pallas_call(write_kernel, out_shape=jax.ShapeDtypeStruct((slides, pair...  1.69 us

profile of v4, /device:TPU:1, one launch (start us, length us, event | category | flops | bytes accessed | tf_op | source)
XLA Modules:
  0.0 26.1 jit_solution(3968629173160578645)
XLA Ops:
  0.0 24.4 %blocks.1.held = bf16[3,4,2,128,512]{4,3,2,1,0:T(8,128)(2,1)S(1)} custom-call(bf16[6,4,2,128,512]{4,3,2,1,0:T(8,128)(2,1)} %bitcast.2, s32[6,64]{1,0:T(8,128)} %tissue_list.1, s32[6]{0:T(128)} %tissue_count.1, bf16[1,512,128]{2,1,0:T(8,128)(2,1)} %w_reduce.1, bf16[1,3,3,128,128]{4,3,2,1,0:T(8,128)(2,1)} %w_spatial.1, bf16[1,128,512]{2,1,0:T(8,128)(2,1)} %w_expand.1, ...), custom_call_target="tpu_custom_call" | custom-call | tf_op jit(solution)/shard_map/blocks/pallas_call | solution.py:569
  24.4 1.7 %write.1 = bf16[3,4,2,128,512]{4,3,2,1,0:T(8,128)(2,1)} custom-call(bf16[3,4,2,128,512]{4,3,2,1,0:T(8,128)(2,1)S(1)} %blocks.1.held), custom_call_target="tpu_custom_call" | custom-call | tf_op jit(solution)/shard_map/write/pallas_call | solution.py:626

commit v5 on v4

--- a/solution.py
+++ b/solution.py
@@ -115,6 +115,7 @@
     lines_recv,
     diag_send,
     diag_recv,
+    fixed,
     rows_ready,
     cols_ready,
     img_sem,
@@ -482,17 +483,15 @@
         done = jnp.concatenate([done, jnp.zeros((128 - strips * 16, chans), BF16)], axis=0)
         for i in range(strips):
             put = jnp.dot(scatter[i], done, preferred_element_type=F32).reshape(pairs, 2, 16, chans)
-            spot = lax.broadcasted_iota(jnp.int32, put.shape, 2)
-            here = out.at[i // 2, :, :, i % 2 * (cols - 16) : i % 2 * (cols - 16) + 16]
-            edges = spot >= 14 if i % 2 else spot < 2
-            here[...] = jnp.where(edges, put, here[...].astype(F32)).astype(BF16)
-
-    late = lax.rem(col, RUN) == 0
+            fixed[i] = put.astype(BF16)
+
+    turn = lax.rem(col, RUN)
+    late, soon = turn == 0, turn == RUN - 1
     for load in own[9:]:
         load.wait()
     for s in range(slides):
         image_load(s).wait()
-    pl.when(jnp.logical_not(late))(send_edges)
+    pl.when(soon)(send_edges)
 
     own[0].wait()
     for copy in swaps[:2]:
@@ -516,6 +515,7 @@
 
     reduce_ends(0, img)
     reduce_between(0, img)
+    pl.when((turn > 0) & (turn < RUN - 1))(send_edges)
 
     for load in own[1:3]:
         load.wait()
@@ -534,12 +534,16 @@
     halo(0)
     expand_pairs(0, ends, img, mid)
     reduce_ends(1, mid)
+    pl.when(late)(send_edges)
     expand_pairs(1, between, mid, out)
+    edge_strips()
     halo(1)
     expand_pairs(1, ends, mid, out)
-
-    pl.when(late)(send_edges)
-    edge_strips()
+    for i in range(2 * slides):
+        place = lax.broadcasted_iota(jnp.int32, (pairs, 2, 16, chans), 2)
+        here = out.at[i // 2, :, :, i % 2 * (cols - 16) : i % 2 * (cols - 16) + 16]
+        edges = place >= 14 if i % 2 else place < 2
+        here[...] = jnp.where(edges, fixed[i].astype(F32), here[...].astype(F32)).astype(BF16)
     for there, copy, _ in edge_sends():
         pl.when(there)(copy.wait_send)
 
@@ -590,6 +594,7 @@
             *[pltpu.VMEM(x.shape, BF16) for x in picks],
             *[pltpu.VMEM((2, slides, 16, chans), BF16)] * 4,
             *[pltpu.VMEM((2, 2, 2, 16, chans), BF16)] * 2,
+            pltpu.VMEM((2 * slides, pairs, 2, 16, chans), BF16),
             pltpu.SemaphoreType.REGULAR,
             pltpu.SemaphoreType.REGULAR,
             dma((slides,)),

time: 26.2 us -> 22.5 us (0.86)
  Pallas kernels: 26.1 us -> 22.5 us
    pallas_call x1, Pallas kernels: 24.4 us -> 20.8 us  [shards(): pl.pallas_call(functools.partial(blocks_kernel, grid), out_shape=pltpu.VM...]
where the time goes in v5:
time: 22.5 us
  Pallas kernels  22.5 us (100%)
    pallas_call x1, Pallas kernels, shards(): pl.pallas_call(functools.partial(blocks_kernel, grid), out_shape=pltpu.VM...  20.8 us
    pallas_call x1, Pallas kernels, shards(): pl.pallas_call(write_kernel, out_shape=jax.ShapeDtypeStruct((slides, pair...  1.69 us

profile of v5, /device:TPU:1, one launch (start us, length us, event | category | flops | bytes accessed | tf_op | source)
XLA Modules:
  0.0 22.5 jit_solution(8693662790141142890)
XLA Ops:
  0.0 20.8 %blocks.1.held = bf16[3,4,2,128,512]{4,3,2,1,0:T(8,128)(2,1)S(1)} custom-call(bf16[6,4,2,128,512]{4,3,2,1,0:T(8,128)(2,1)} %bitcast.2, s32[6,64]{1,0:T(8,128)} %tissue_list.1, s32[6]{0:T(128)} %tissue_count.1, bf16[1,512,128]{2,1,0:T(8,128)(2,1)} %w_reduce.1, bf16[1,3,3,128,128]{4,3,2,1,0:T(8,128)(2,1)} %w_spatial.1, bf16[1,128,512]{2,1,0:T(8,128)(2,1)} %w_expand.1, ...), custom_call_target="tpu_custom_call" | custom-call | tf_op jit(solution)/shard_map/blocks/pallas_call | solution.py:573
  20.8 1.7 %write.1 = bf16[3,4,2,128,512]{4,3,2,1,0:T(8,128)(2,1)} custom-call(bf16[3,4,2,128,512]{4,3,2,1,0:T(8,128)(2,1)S(1)} %blocks.1.held), custom_call_target="tpu_custom_call" | custom-call | tf_op jit(solution)/shard_map/write/pallas_call | solution.py:631

commit v6 on v5

--- a/solution.py
+++ b/solution.py
@@ -371,7 +371,7 @@
         for there, copy, _ in edge_sends():
             pl.when(there)(copy.start)
 
-    def edge_strips():
+    def edge_wait():
         copies = list(edge_sends())
         for n, (there, _, here) in enumerate(copies):
             pl.when(there)(copies[mirror(n)][1].wait_recv)
@@ -380,6 +380,7 @@
             def _():
                 here[...] = jnp.zeros_like(here)
 
+    def edge_strips():
         strips = 2 * slides
         own_row = lax.broadcasted_iota(jnp.int32, (16, inner), 0)
         valid = jnp.where(
@@ -536,9 +537,20 @@
     reduce_ends(1, mid)
     pl.when(late)(send_edges)
     expand_pairs(1, between, mid, out)
-    edge_strips()
+
+    @pl.when(jnp.logical_not(late))
+    def _():
+        edge_wait()
+        edge_strips()
+
     halo(1)
     expand_pairs(1, ends, mid, out)
+
+    @pl.when(late)
+    def _():
+        edge_wait()
+        edge_strips()
+
     for i in range(2 * slides):
         place = lax.broadcasted_iota(jnp.int32, (pairs, 2, 16, chans), 2)
         here = out.at[i // 2, :, :, i % 2 * (cols - 16) : i % 2 * (cols - 16) + 16]

time: 22.5 us -> 21.6 us (0.960)
  Pallas kernels: 22.5 us -> 21.5 us
    pallas_call x1, Pallas kernels: 20.8 us -> 19.8 us  [shards(): pl.pallas_call(functools.partial(blocks_kernel, grid), out_shape=pltpu.VM...]
where the time goes in v6:
time: 21.6 us; the launch traced here: 21.5 us
  Pallas kernels  21.5 us (100%)
    pallas_call x1, Pallas kernels, shards(): pl.pallas_call(functools.partial(blocks_kernel, grid), out_shape=pltpu.VM...  19.8 us
    pallas_call x1, Pallas kernels, shards(): pl.pallas_call(write_kernel, out_shape=jax.ShapeDtypeStruct((slides, pair...  1.69 us

profile of v6, /device:TPU:1, one launch (start us, length us, event | category | flops | bytes accessed | tf_op | source)
XLA Modules:
  0.0 21.5 jit_solution(4368749674383137157)
XLA Ops:
  0.0 19.8 %blocks.1.held = bf16[3,4,2,128,512]{4,3,2,1,0:T(8,128)(2,1)S(1)} custom-call(bf16[6,4,2,128,512]{4,3,2,1,0:T(8,128)(2,1)} %bitcast.2, s32[6,64]{1,0:T(8,128)} %tissue_list.1, s32[6]{0:T(128)} %tissue_count.1, bf16[1,512,128]{2,1,0:T(8,128)(2,1)} %w_reduce.1, bf16[1,3,3,128,128]{4,3,2,1,0:T(8,128)(2,1)} %w_spatial.1, bf16[1,128,512]{2,1,0:T(8,128)(2,1)} %w_expand.1, ...), custom_call_target="tpu_custom_call" | custom-call | tf_op jit(solution)/shard_map/blocks/pallas_call | solution.py:585
  19.8 1.7 %write.1 = bf16[3,4,2,128,512]{4,3,2,1,0:T(8,128)(2,1)} custom-call(bf16[3,4,2,128,512]{4,3,2,1,0:T(8,128)(2,1)S(1)} %blocks.1.held), custom_call_target="tpu_custom_call" | custom-call | tf_op jit(solution)/shard_map/write/pallas_call | solution.py:643

commit v7 on v6

--- a/solution.py
+++ b/solution.py
@@ -492,7 +492,6 @@
         load.wait()
     for s in range(slides):
         image_load(s).wait()
-    pl.when(soon)(send_edges)
 
     own[0].wait()
     for copy in swaps[:2]:
@@ -516,7 +515,7 @@
 
     reduce_ends(0, img)
     reduce_between(0, img)
-    pl.when((turn > 0) & (turn < RUN - 1))(send_edges)
+    pl.when(soon)(send_edges)
 
     for load in own[1:3]:
         load.wait()
@@ -531,6 +530,7 @@
             expand(e, sp, p, before, after)
 
     expand_pairs(0, between, img, mid)
+    pl.when((turn > 0) & (turn < RUN - 1))(send_edges)
     reduce_between(1, mid)
     halo(0)
     expand_pairs(0, ends, img, mid)

time: 21.6 us -> 22.1 us (1.023)
  Pallas kernels: 21.5 us -> 22 us
    pallas_call x1, Pallas kernels: 19.8 us -> 20.3 us  [shards(): pl.pallas_call(functools.partial(blocks_kernel, grid), out_shape=pltpu.VM...]
where the time goes in v7:
time: 22.1 us; the launch traced here: 22 us
  Pallas kernels  22 us (100%)
    pallas_call x1, Pallas kernels, shards(): pl.pallas_call(functools.partial(blocks_kernel, grid), out_shape=pltpu.VM...  20.3 us
    pallas_call x1, Pallas kernels, shards(): pl.pallas_call(write_kernel, out_shape=jax.ShapeDtypeStruct((slides, pair...  1.69 us

profile of v7, /device:TPU:1, one launch (start us, length us, event | category | flops | bytes accessed | tf_op | source)
XLA Modules:
  0.0 22.0 jit_solution(18216961927853007514)
XLA Ops:
  0.0 20.3 %blocks.1.held = bf16[3,4,2,128,512]{4,3,2,1,0:T(8,128)(2,1)S(1)} custom-call(bf16[6,4,2,128,512]{4,3,2,1,0:T(8,128)(2,1)} %bitcast.2, s32[6,64]{1,0:T(8,128)} %tissue_list.1, s32[6]{0:T(128)} %tissue_count.1, bf16[1,512,128]{2,1,0:T(8,128)(2,1)} %w_reduce.1, bf16[1,3,3,128,128]{4,3,2,1,0:T(8,128)(2,1)} %w_spatial.1, bf16[1,128,512]{2,1,0:T(8,128)(2,1)} %w_expand.1, ...), custom_call_target="tpu_custom_call" | custom-call | tf_op jit(solution)/shard_map/blocks/pallas_call | solution.py:585
  20.3 1.7 %write.1 = bf16[3,4,2,128,512]{4,3,2,1,0:T(8,128)(2,1)} custom-call(bf16[3,4,2,128,512]{4,3,2,1,0:T(8,128)(2,1)S(1)} %blocks.1.held), custom_call_target="tpu_custom_call" | custom-call | tf_op jit(solution)/shard_map/write/pallas_call | solution.py:643

commit v8 on v7

--- a/solution.py
+++ b/solution.py
@@ -301,11 +301,14 @@
         for way, there, r in ((0, row > 0, -1), (1, row < n_row - 1, 2 * pairs)):
             place_row(e, r, jnp.where(there, row_recv[e, way].astype(F32), 0.0))
 
-    def spatial(e, p):
-        total = jnp.dot(rb[e, :, p].reshape(-1, 6 * inner), wa[e], preferred_element_type=F32)
-        total += jnp.dot(rb[e, :, p + 1].reshape(-1, 6 * inner), wb[e], preferred_element_type=F32)
+    def spatial_part(e, p, w, i):
+        return jnp.dot(rb[e, :, p + i].reshape(-1, 6 * inner), w[e], preferred_element_type=F32)
+
+    def spatial(e, p, first=None, second=None):
+        first = spatial_part(e, p, wa, 0) if first is None else first
+        second = spatial_part(e, p, wb, 1) if second is None else second
         gain, bias = widen(gb[e, 1:2], 2), widen(gb[e, 3:4], 2)
-        return jnp.maximum(total * gain + bias, 0.0).astype(BF16)
+        return jnp.maximum((first + second) * gain + bias, 0.0).astype(BF16)
 
     def expand(e, sp, p, before, after):
         gain, bias = outer(e)
@@ -492,6 +495,7 @@
         load.wait()
     for s in range(slides):
         image_load(s).wait()
+    pl.when(soon)(send_edges)
 
     own[0].wait()
     for copy in swaps[:2]:
@@ -515,7 +519,6 @@
 
     reduce_ends(0, img)
     reduce_between(0, img)
-    pl.when(soon)(send_edges)
 
     for load in own[1:3]:
         load.wait()
@@ -529,24 +532,31 @@
         for p, sp in zip(group, parts):
             expand(e, sp, p, before, after)
 
+    def expand_ends(e, before, after):
+        top, bottom = ends
+        below = spatial_part(e, top, wb, 1)
+        above = spatial_part(e, bottom, wa, 0)
+        halo(e)
+        parts = [spatial(e, top, second=below), spatial(e, bottom, first=above)]
+        for p, sp in zip(ends, parts):
+            expand(e, sp, p, before, after)
+
     expand_pairs(0, between, img, mid)
     pl.when((turn > 0) & (turn < RUN - 1))(send_edges)
     reduce_between(1, mid)
-    halo(0)
-    expand_pairs(0, ends, img, mid)
+    expand_ends(0, img, mid)
     reduce_ends(1, mid)
     pl.when(late)(send_edges)
     expand_pairs(1, between, mid, out)
 
-    @pl.when(jnp.logical_not(late))
+    @pl.when(turn > 1)
     def _():
         edge_wait()
         edge_strips()
 
-    halo(1)
-    expand_pairs(1, ends, mid, out)
-
-    @pl.when(late)
+    expand_ends(1, mid, out)
+
+    @pl.when(turn <= 1)
     def _():
         edge_wait()
         edge_strips()

time: 22.1 us -> 20.5 us (0.928)
  Pallas kernels: 22 us -> 20.4 us
    pallas_call x1, Pallas kernels: 20.3 us -> 18.7 us  [shards(): pl.pallas_call(functools.partial(blocks_kernel, grid), out_shape=pltpu.VM...]
where the time goes in v8:
time: 20.5 us; the launch traced here: 20.4 us
  Pallas kernels  20.4 us (100%)
    pallas_call x1, Pallas kernels, shards(): pl.pallas_call(functools.partial(blocks_kernel, grid), out_shape=pltpu.VM...  18.7 us
    pallas_call x1, Pallas kernels, shards(): pl.pallas_call(write_kernel, out_shape=jax.ShapeDtypeStruct((slides, pair...  1.69 us

profile of v8, /device:TPU:1, one launch (start us, length us, event | category | flops | bytes accessed | tf_op | source)
XLA Modules:
  0.0 20.4 jit_solution(10931308017729812214)
XLA Ops:
  0.0 18.7 %blocks.1.held = bf16[3,4,2,128,512]{4,3,2,1,0:T(8,128)(2,1)S(1)} custom-call(bf16[6,4,2,128,512]{4,3,2,1,0:T(8,128)(2,1)} %bitcast.2, s32[6,64]{1,0:T(8,128)} %tissue_list.1, s32[6]{0:T(128)} %tissue_count.1, bf16[1,512,128]{2,1,0:T(8,128)(2,1)} %w_reduce.1, bf16[1,3,3,128,128]{4,3,2,1,0:T(8,128)(2,1)} %w_spatial.1, bf16[1,128,512]{2,1,0:T(8,128)(2,1)} %w_expand.1, ...), custom_call_target="tpu_custom_call" | custom-call | tf_op jit(solution)/shard_map/blocks/pallas_call | solution.py:595
  18.7 1.7 %write.1 = bf16[3,4,2,128,512]{4,3,2,1,0:T(8,128)(2,1)} custom-call(bf16[3,4,2,128,512]{4,3,2,1,0:T(8,128)(2,1)S(1)} %blocks.1.held), custom_call_target="tpu_custom_call" | custom-call | tf_op jit(solution)/shard_map/write/pallas_call | solution.py:653

commit v9 on v8

--- a/solution.py
+++ b/solution.py
@@ -348,8 +348,7 @@
         cells = img[s, :, :, side * (cols - 16) : side * (cols - 16) + 16]
         return cells.reshape(2 * pairs * 16, chans)
 
-    def send_edges():
-        meet(0, 2 * number(lambda j: j != 0), cols_ready)
+    def gather_edges():
         parts = []
         for s in range(slides):
             parts.append(
@@ -371,6 +370,9 @@
                 for t in range(2):
                     two = [parts[min(2 * t + i, slides - 1)][side][cut] for i in range(2)]
                     diag_send[way, side, t] = jnp.concatenate(two, axis=0).astype(BF16)
+
+    def send_edges():
+        meet(0, 2 * number(lambda j: j != 0), cols_ready)
         for there, copy, _ in edge_sends():
             pl.when(there)(copy.start)
 
@@ -495,6 +497,7 @@
         load.wait()
     for s in range(slides):
         image_load(s).wait()
+    gather_edges()
     pl.when(soon)(send_edges)
 
     own[0].wait()

time: 20.5 us -> 20.5 us (level); the launches traced: 20.4 us -> 20.1 us
  Pallas kernels: 20.4 us -> 20.1 us
    pallas_call x1, Pallas kernels: 18.7 us -> 18.4 us  [shards(): pl.pallas_call(functools.partial(blocks_kernel, grid), out_shape=pltpu.VM...]
where the time goes in v9:
time: 20.5 us; the launch traced here: 20.1 us
  Pallas kernels  20.1 us (98%)
    pallas_call x1, Pallas kernels, shards(): pl.pallas_call(functools.partial(blocks_kernel, grid), out_shape=pltpu.VM...  18.4 us
    pallas_call x1, Pallas kernels, shards(): pl.pallas_call(write_kernel, out_shape=jax.ShapeDtypeStruct((slides, pair...  1.69 us

profile of v9, /device:TPU:1, one launch (start us, length us, event | category | flops | bytes accessed | tf_op | source)
XLA Modules:
  0.0 20.1 jit_solution(8239543465517084417)
XLA Ops:
  0.0 18.4 %blocks.1.held = bf16[3,4,2,128,512]{4,3,2,1,0:T(8,128)(2,1)S(1)} custom-call(bf16[6,4,2,128,512]{4,3,2,1,0:T(8,128)(2,1)} %bitcast.2, s32[6,64]{1,0:T(8,128)} %tissue_list.1, s32[6]{0:T(128)} %tissue_count.1, bf16[1,512,128]{2,1,0:T(8,128)(2,1)} %w_reduce.1, bf16[1,3,3,128,128]{4,3,2,1,0:T(8,128)(2,1)} %w_spatial.1, bf16[1,128,512]{2,1,0:T(8,128)(2,1)} %w_expand.1, ...), custom_call_target="tpu_custom_call" | custom-call | tf_op jit(solution)/shard_map/blocks/pallas_call | solution.py:598
  18.4 1.7 %write.1 = bf16[3,4,2,128,512]{4,3,2,1,0:T(8,128)(2,1)} custom-call(bf16[3,4,2,128,512]{4,3,2,1,0:T(8,128)(2,1)S(1)} %blocks.1.held), custom_call_target="tpu_custom_call" | custom-call | tf_op jit(solution)/shard_map/write/pallas_call | solution.py:656
